TPU v7x, 32 devices: a whole 2x2x4 slice. The times are simulated.
32 devices in a mesh: section: 4 (over y, x), dp: 8 (over z, core).
Axes of the slice: x: 2, y: 2, z: 4, core: 2. Of those that a mesh axis runs over, the one named last changes fastest.
Arguments:
- tokens: bfloat16 [96, 237, 768], P(('section', 'dp')), may hold values from -6 to 6
- caption_lengths: int32 [96], P(('section', 'dp')), may hold values from 8 to 40, as said below
- attend_gain: float32 [4, 768], P('section'), may hold values from 0.5 to 1.5
- attend_shift: float32 [4, 768], P('section'), may hold values from -1.25 to 1.25
- attend_inputs: bfloat16 [4, 768, 2304], P('section'), may hold values from -0.21875 to 0.21875
- attend_bias: float32 [4, 2304], P('section'), may hold values from -1.25 to 1.25
- attend_output: bfloat16 [4, 768, 768], P('section'), may hold values from -1.75 to 1.75
- expert_gain: float32 [4, 768], P('section'), may hold values from 0.5 to 1.5
- expert_shift: float32 [4, 768], P('section'), may hold values from -1.25 to 1.25
- expert_inputs: bfloat16 [4, 768, 3072], P('section'), may hold values from -0.21875 to 0.21875
- expert_inner_bias: float32 [4, 3072], P('section'), may hold values from -1.75 to 1.75
- expert_outputs: bfloat16 [4, 3072, 768], P('section'), may hold values from -0.109375 to 0.109375
- expert_outer_bias: float32 [4, 768], P('section'), may hold values from -1.25 to 1.25
- cotangent: bfloat16 [96, 237, 768], P(('section', 'dp')), may hold values from -6 to 6
Outputs:
- layer_output: bfloat16 [96, 237, 768], P(('section', 'dp'))
- tokens_grad: bfloat16 [96, 237, 768], P(('section', 'dp'))
- attend_gain_grad: float32 [4, 768], P('section')
- attend_shift_grad: float32 [4, 768], P('section')
- attend_inputs_grad: float32 [4, 768, 2304], P('section')
- attend_bias_grad: float32 [4, 2304], P('section')
- attend_output_grad: float32 [4, 768, 768], P('section')
- expert_gain_grad: float32 [4, 768], P('section')
- expert_shift_grad: float32 [4, 768], P('section')
- expert_inputs_grad: float32 [4, 768, 3072], P('section')
- expert_inner_bias_grad: float32 [4, 3072], P('section')
- expert_outputs_grad: float32 [4, 3072, 768], P('section')
- expert_outer_bias_grad: float32 [4, 768], P('section')
- expert_counts: int32 [3], replicated
Inputs may be any that keep to these rules, and one draw needn't show every extreme that they name: `caption_lengths`: number of true caption tokens of an item; the rest of its 40 caption slots is padding.
All inputs are finite; a program needn't handle non-finite values.
Results may differ from a plain program's by a relative error of at most 0.02.
Values may be sent and summed in bfloat16 or wider, within the bound.
No kernel may reach another device: no remote copies, remote signals or barrier semaphores. Data moves between devices by JAX's collectives and lax.ppermute only.
A program may use at most 256 MiB of HBM per device.

v0:
```python
from functools import partial

import jax
import jax.numpy as jnp
from jax import lax
from jax.experimental import pallas as pl
from jax.experimental.pallas import tpu as pltpu
from jax.sharding import Mesh
from jax.sharding import PartitionSpec as P

HEADS = 12
HEAD_DIM = 64
PATCHES = 197
ROWS = 256
CAP_FIRST, CAP_ROWS = 192, 48
PATCH_ROWS = 208
PAIR = 2 * HEAD_DIM
SECTIONS = 4
PIECE_ROWS = 48
VMEM_BYTES = 58 * 1024 * 1024
F32 = jnp.float32
BF16 = jnp.bfloat16

PLAN_FOUR = (
    ({0: "a0", 1: "e0", 2: "c0", 3: "F"}, {0: "a1", 1: "e2", 2: "c0", 3: "F"}),
    ({0: "a1", 1: "e1", 2: "a1", 3: "e2"}, {0: "a0", 1: "a0", 2: "F", 3: "c0"}),
    ({0: "g3", 1: "e2", 2: "c1"}, {0: "e0", 1: "e3", 2: "c1"}),
    ({0: "g1", 1: "e3", 2: "e0", 3: "e3"}, {0: "e1", 1: "e1", 3: "c1"}),
    ({}, {0: "g2", 1: "g3"}),
)
PLAN_ANY = (
    ({0: "a0", 1: "e0", 2: "c0", 3: "f0"}, {0: "a1", 1: "e2", 2: "c0", 3: "f0"}),
    ({0: "a1", 1: "e1", 2: "a1", 3: "e2"}, {0: "a0", 1: "a0", 2: "c1", 3: "f1"}),
    ({0: "g3", 1: "e2", 2: "c1", 3: "f1"}, {0: "e0", 1: "e3", 2: "f0", 3: "f2"}),
    ({0: "g1", 1: "e3", 2: "e0", 3: "e3"}, {0: "e1", 1: "e1", 2: "f1", 3: "f3"}),
    ({0: "c1", 1: "f2", 3: "f2"}, {0: "g2", 1: "g3", 3: "c0"}),
    ({1: "f3", 3: "f3"}, {}),
)
HOMES = {"a": 0, "c": 2, "e": 1, "f": 3, "F": 3, "g": 0}
ATTEND_BLOCKS = ((0, 1), (2, 3))
EXPERT_BLOCKS = ((0, 1), (4, 5), (2, 3), (6, 7))


def dot_plain(left, right):
    return jnp.dot(left, right, preferred_element_type=F32)


def dot_last(left, right):
    return lax.dot_general(left, right, (((1,), (1,)), ((), ())), preferred_element_type=F32)


def dot_first(left, right):
    return lax.dot_general(left, right, (((0,), (0,)), ((), ())), preferred_element_type=F32)


def column_sum(matrix):
    return jnp.sum(matrix.astype(F32), axis=0, keepdims=True)


def norm_parts(rows):
    centre = rows - jnp.mean(rows, axis=-1, keepdims=True)
    scale = lax.rsqrt(jnp.mean(centre * centre, axis=-1, keepdims=True) + 1e-06)
    return centre * scale, scale


def norm_back(normed_grad, unit, scale, gain):
    unit_grad = normed_grad * gain
    along = jnp.mean(unit_grad * unit, axis=-1, keepdims=True)
    return scale * (unit_grad - jnp.mean(unit_grad, axis=-1, keepdims=True) - unit * along)


def true_positions(length, first, count, axis, kind):
    shape = (count, 1) if axis == 0 else (1, count)
    position = first + lax.broadcasted_iota(jnp.int32, shape, axis)
    patch = position < PATCHES
    if kind == "patch":
        return patch
    caption = (position >= PATCHES) & (position - PATCHES < length)
    return caption if kind == "caption" else patch | caption


def head_masks():
    lane = lax.broadcasted_iota(jnp.int32, (1, PAIR), 1)
    even = (lane < HEAD_DIM).astype(F32).astype(BF16)
    odd = (lane >= HEAD_DIM).astype(F32).astype(BF16)
    return lane < HEAD_DIM, even, odd


def split_pair(pair, even, odd):
    return jnp.concatenate([pair * even, pair * odd], axis=0)


def start_weights(info, first, refs, plan, blocks, sems):
    half = blocks.shape[1] // 2
    section, core, plane = info[first], info[first + 1], info[first + 2]
    for at, at_plane, steps in plan:
        here = section == at
        if at_plane is not None:
            here = here & (plane == at_plane)

        @pl.when(here)
        def _(steps=steps):
            for block, source in steps:
                if source[0] == "own":
                    _, which, row, column = source
                    width = blocks.shape[2]
                    for part in range(2):
                        pltpu.make_async_copy(
                            refs[which].at[
                                pl.ds(row + part * half, half), pl.ds(column, width)
                            ],
                            blocks.at[block, pl.ds(part * half, half)],
                            sems.at[block],
                        ).start()
                else:
                    _, mine, theirs, index = source
                    pltpu.make_async_copy(
                        refs[mine].at[index],
                        blocks.at[block, pl.ds(pl.multiple_of(core * half, half), half)],
                        sems.at[block],
                    ).start()
                    pltpu.make_async_copy(
                        refs[theirs].at[index],
                        blocks.at[block, pl.ds(pl.multiple_of((1 - core) * half, half), half)],
                        sems.at[block],
                    ).start()


def wait_block(blocks, block, sems):
    pltpu.make_async_copy(blocks.at[block], blocks.at[block], sems.at[block]).wait()


def store_turned(target, turned, columns, section, core):
    half = target.shape[0] // 2
    for piece in range(16):
        path, owner = (piece >> 2) & 1, piece & 3
        away = owner ^ section
        place = ((away & 1) << 1) | (away >> 1) if path == 0 else away
        row = ((piece >> 3) ^ core) * half + (place >> 1) * (half // 2)
        row = row + path * (half // 4) + (place & 1) * PIECE_ROWS
        target[pl.ds(pl.multiple_of(row, 16), PIECE_ROWS), columns] = turned[
            piece * PIECE_ROWS : (piece + 1) * PIECE_ROWS
        ]


def put_travel(refs, which, columns, left, right):
    half = left.shape[0] // 2
    for side in range(2):
        rows = dot_plain(left[side * half : (side + 1) * half], right).astype(BF16)
        refs[2 * side][which, :, columns] = rows[: half // 2]
        refs[2 * side + 1][which, :, columns] = rows[half // 2 :]


def attend_forward_kernel(plan, weight_count, merge, info, *refs):
    weights, refs = refs[:weight_count], refs[weight_count:]
    if merge:
        x_ref, before_ref, part_ref, outer_ref, gain_ref, shift_ref, bias_ref = refs[:7]
        y_ref, qkv_ref, mixed_ref, joined_ref, blocks, sems, joined = refs[7:]
    else:
        x_ref, gain_ref, shift_ref, bias_ref, next_gain_ref, next_shift_ref = refs[:6]
        y_ref, qkv_ref, mixed_ref, caption_ref, blocks, sems = refs[6:]
    item = pl.program_id(0)
    items = pl.num_programs(0)
    length = info[item]
    width = x_ref.shape[-1]

    @pl.when(item == 0)
    def _():
        start_weights(info, items, weights, plan, blocks, sems)

    cap = slice(CAP_FIRST, CAP_FIRST + CAP_ROWS)
    if merge:
        joined[...] = x_ref[0].astype(F32)
        branch = part_ref[0].astype(F32) + outer_ref[...]
        is_true = true_positions(length, CAP_FIRST, CAP_ROWS, 0, "caption")
        captions = before_ref[0, cap] + jnp.where(is_true, branch, 0.0)
        position = CAP_FIRST + lax.broadcasted_iota(jnp.int32, (CAP_ROWS, 1), 0)
        captions = captions.astype(BF16).astype(F32)
        joined[cap] = jnp.where(position < PATCHES, joined[cap], captions)
        x = joined[...]
        joined_ref[0] = x.astype(BF16)
    else:
        x = x_ref[0].astype(F32)
    unit, _ = norm_parts(x)
    normed = (unit * gain_ref[...] + shift_ref[...]).astype(BF16)

    @pl.when(item == 0)
    def _():
        for block in range(4):
            wait_block(blocks, block, sems)

    queries = dot_plain(normed, blocks[0]) + bias_ref[:, :width]
    qkv_ref[0, :, :width] = (queries * HEAD_DIM ** (-0.5)).astype(BF16)
    qkv_ref[0, :, width : 2 * width] = dot_plain(normed, blocks[1]).astype(BF16)
    values = dot_plain(normed, blocks[2]) + bias_ref[:, width : 2 * width]
    qkv_ref[0, :, 2 * width :] = values.astype(BF16)
    key_true = true_positions(length, 0, ROWS, 1, "all")
    low_half, even, odd = head_masks()
    ones = jnp.ones((ROWS, PAIR), BF16)

    def scores_of(pair):
        at = pair * PAIR
        q2 = qkv_ref[0, :, at : at + PAIR]
        k2 = qkv_ref[0, :, width + at : width + at + PAIR]
        return dot_last(split_pair(q2, even, odd), k2)

    ahead = [scores_of(0), scores_of(1)]
    for pair in range(HEADS // 2):
        at = pair * PAIR
        scores = jnp.where(key_true, ahead.pop(0), -1e9)
        if pair + 2 < HEADS // 2:
            ahead.append(scores_of(pair + 2))
        weight = jnp.exp(scores - jnp.max(scores, axis=-1, keepdims=True)).astype(BF16)
        v2 = qkv_ref[0, :, 2 * width + at : 2 * width + at + PAIR]
        summed = dot_plain(weight, jnp.concatenate([v2, ones], axis=1))
        top = jnp.where(low_half, summed[:ROWS, :PAIR], summed[ROWS:, :PAIR])
        below = jnp.where(low_half, summed[:ROWS, PAIR:], summed[ROWS:, PAIR:])
        mixed_ref[0, :, at : at + PAIR] = (top / below).astype(BF16)
    branch = dot_plain(mixed_ref[0], blocks[3]) + bias_ref[:, 2 * width :]
    row_true = true_positions(length, 0, ROWS, 0, "all")
    y = x + jnp.where(row_true, branch, 0.0)
    y_ref[0] = y.astype(y_ref.dtype)
    if not merge:
        unit, _ = norm_parts(y[cap])
        caption_ref[0] = (unit * next_gain_ref[...] + next_shift_ref[...]).astype(BF16)


def attend_backward_kernel(plan, weight_count, first, info, *refs):
    weights, refs = refs[:weight_count], refs[weight_count:]
    x_ref, gain_ref, shift_ref, qkv_ref, mixed_ref, grad_ref = refs[:6]
    if first:
        after_ref, next_gain_ref, *parts = refs[6:12]
        refs = refs[12:]
    else:
        refs = refs[6:]
    out_ref, gain_grad_ref, shift_grad_ref, bias_grad_ref = refs[:4]
    travel_refs = refs[4:8]
    if first:
        next_gain_grad_ref, next_shift_grad_ref, joined = refs[8], refs[9], refs[-1]
    else:
        caption_ref = refs[8]
    blocks, sems, normed_turned, mixed_turned, branch_all, projected, mixed_grad = refs[
        10 if first else 9 :
    ][:7]
    item = pl.program_id(0)
    items = pl.num_programs(0)
    length = info[item]
    section, core = info[items], info[items + 1]
    width = x_ref.shape[-1]
    here = pl.ds(pl.multiple_of(item * ROWS, ROWS), ROWS)
    cap = slice(CAP_FIRST, CAP_FIRST + CAP_ROWS)

    @pl.when(item == 0)
    def _():
        start_weights(info, items, weights, plan, blocks, sems)

    def add_to(ref, part):
        @pl.when(item == 0)
        def _():
            ref[...] = part

        @pl.when(item > 0)
        def _():
            ref[...] += part

    x = x_ref[0].astype(F32)
    unit, scale = norm_parts(x)
    normed = (unit * gain_ref[...] + shift_ref[...]).astype(BF16)
    incoming = grad_ref[0].astype(F32)
    if first:
        after_unit, after_scale = norm_parts(after_ref[0, cap])
        caption_grad = parts[0][...].astype(F32)
        for part in parts[1:]:
            caption_grad = caption_grad + part[...].astype(F32)
        joined[...] = incoming
        joined[cap] += norm_back(caption_grad, after_unit, after_scale, next_gain_ref[...])
        incoming = joined[...]
        add_to(next_gain_grad_ref, jnp.sum(caption_grad * after_unit, axis=0, keepdims=True))
        add_to(next_shift_grad_ref, jnp.sum(caption_grad, axis=0, keepdims=True))
    row_true = true_positions(length, 0, ROWS, 0, "all")
    branch = jnp.where(row_true, incoming, 0.0).astype(BF16)
    branch_all[here, :] = branch
    store_turned(normed_turned, normed.T, here, section, core)
    store_turned(mixed_turned, mixed_ref[0].T, here, section, core)

    @pl.when(item == 0)
    def _():
        for block in range(4):
            wait_block(blocks, block, sems)

    mixed_grad[...] = dot_last(branch, blocks[3]).astype(BF16)
    key_true = true_positions(length, 0, ROWS, 0, "all")
    _, even, odd = head_masks()

    def products_of(pair):
        at = pair * PAIR
        q2 = split_pair(qkv_ref[0, :, at : at + PAIR], even, odd)
        k2 = qkv_ref[0, :, width + at : width + at + PAIR]
        v2 = qkv_ref[0, :, 2 * width + at : 2 * width + at + PAIR]
        g2 = split_pair(mixed_grad[:, at : at + PAIR], even, odd)
        return q2, k2, g2, dot_last(k2, q2), dot_last(v2, g2)

    ahead = [products_of(0)]
    for pair in range(HEADS // 2):
        at = pair * PAIR
        q2, k2, g2, scores, weight_grad = ahead.pop(0)
        if pair + 1 < HEADS // 2:
            ahead.append(products_of(pair + 1))
        scores = jnp.where(key_true, scores, -1e9)
        weight = jnp.exp(scores - jnp.max(scores, axis=0, keepdims=True))
        weight = weight * (1.0 / jnp.sum(weight, axis=0, keepdims=True))
        product = weight * weight_grad
        along = jnp.sum(product, axis=0, keepdims=True)
        score_grad = (product - weight * along).astype(BF16)
        values_grad = dot_plain(weight.astype(BF16), g2).astype(BF16)
        keys_grad = dot_plain(score_grad, q2).astype(BF16)
        k2_split = split_pair(k2, even, odd)
        stacked = jnp.concatenate([score_grad[:, :ROWS], score_grad[:, ROWS:]], axis=0)
        queries_grad = dot_first(stacked, k2_split).astype(BF16)
        queries_grad = (queries_grad.astype(F32) * HEAD_DIM ** (-0.5)).astype(BF16)
        projected[here, at : at + PAIR] = queries_grad
        projected[here, width + at : width + at + PAIR] = keys_grad
        projected[here, 2 * width + at : 2 * width + at + PAIR] = values_grad
    normed_grad = dot_last(projected[here, :width], blocks[0])
    normed_grad += dot_last(projected[here, width : 2 * width], blocks[1])
    normed_grad += dot_last(projected[here, 2 * width :], blocks[2])
    out = (incoming + norm_back(normed_grad, unit, scale, gain_ref[...])).astype(BF16)
    out_ref[0] = out
    if not first:
        is_true = true_positions(length, CAP_FIRST, CAP_ROWS, 0, "caption")
        caption_ref[0] = jnp.where(is_true, out[cap].astype(F32), 0.0).astype(BF16)
    add_to(gain_grad_ref, jnp.sum(normed_grad * unit, axis=0, keepdims=True))
    add_to(shift_grad_ref, jnp.sum(normed_grad, axis=0, keepdims=True))

    @pl.when(item == items - 1)
    def _():
        for block in range(4):
            columns = slice(block * width, (block + 1) * width)
            left = normed_turned if block < 3 else mixed_turned
            right = projected[:, columns] if block < 3 else branch_all[...]
            put_travel(travel_refs, 0, columns, left, right)
        bias_grad_ref[:, :width] = column_sum(projected[:, :width])
        bias_grad_ref[:, width : 2 * width] = column_sum(projected[:, 2 * width :])
        bias_grad_ref[:, 2 * width :] = column_sum(branch_all[...])


SHORT = pl.CostEstimate(flops=0, bytes_accessed=100_000, transcendentals=0)
LONG = pl.CostEstimate(flops=30_000_000_000, bytes_accessed=30_000_000, transcendentals=0)
ANYWHERE = pl.BlockSpec(memory_space=pl.ANY)


def whole_block(shape):
    return pl.BlockSpec(shape, lambda step, info: (0,) * len(shape))


def item_block(shape):
    return pl.BlockSpec((1,) + shape[1:], lambda step, info: (step,) + (0,) * (len(shape) - 1))


def blocks_scratch(count, width):
    return [pltpu.VMEM((count, width, width), BF16), pltpu.SemaphoreType.DMA((count,))]


def attend_forward(x, info, weights, gain, shift, bias, merge=None, following=None):
    arrays, plan = weights
    items, _, width = x.shape
    row = whole_block((1, width))
    bias_row = whole_block((1, 3 * width))
    caption_shape = (items, CAP_ROWS, width)
    if merge is not None:
        before, part, outer = merge
        operands = (x, before, part, outer, gain, shift, bias)
        specs = [item_block(x.shape), item_block(x.shape), item_block(caption_shape)]
        specs += [row, row, row, bias_row]
        last_shape, kind, scratch = x.shape, BF16, [pltpu.VMEM((ROWS, width), F32)]
    else:
        operands = (x, gain, shift, bias, *following)
        specs = [item_block(x.shape), row, row, bias_row, row, row]
        last_shape, kind, scratch = caption_shape, F32, []
    return pl.pallas_call(
        partial(attend_forward_kernel, plan, len(arrays), merge is not None),
        grid_spec=pltpu.PrefetchScalarGridSpec(
            num_scalar_prefetch=1,
            grid=(items,),
            in_specs=[ANYWHERE] * len(arrays) + specs,
            out_specs=[
                item_block(x.shape),
                item_block((items, ROWS, 3 * width)),
                item_block((items, ROWS, width)),
                item_block(last_shape),
            ],
            scratch_shapes=blocks_scratch(4, width) + scratch,
        ),
        out_shape=[
            jax.ShapeDtypeStruct(x.shape, kind),
            jax.ShapeDtypeStruct((items, ROWS, 3 * width), BF16),
            jax.ShapeDtypeStruct((items, ROWS, width), BF16),
            jax.ShapeDtypeStruct(last_shape, BF16),
        ],
        compiler_params=pltpu.CompilerParams(vmem_limit_bytes=VMEM_BYTES),
        cost_estimate=SHORT,
        name="attend_forward",
    )(info, *arrays, *operands)


def attend_backward(x, info, weights, gain, shift, qkv, mixed, incoming, first=None):
    arrays, plan = weights
    items, _, width = x.shape
    half = width // 2
    row = whole_block((1, width))
    caption_shape = (items, CAP_ROWS, width)
    operands = (x, gain, shift, qkv, mixed, incoming)
    specs = [item_block(x.shape), row, row, item_block(qkv.shape), item_block(mixed.shape)]
    specs += [item_block(incoming.shape)]
    outs = [
        (item_block(x.shape), x.shape, BF16),
        (row, (1, width), F32),
        (row, (1, width), F32),
        (whole_block((1, 3 * width)), (1, 3 * width), F32),
    ]
    outs += [(whole_block((1, half // 2, 4 * width)), (1, half // 2, 4 * width), BF16)] * 4
    scratch = []
    if first is not None:
        after, next_gain, parts = first
        operands += (after, next_gain, *parts)
        caption_rows = pl.BlockSpec((CAP_ROWS, width), lambda step, info: (step, 0))
        specs += [item_block(after.shape), row] + [caption_rows] * 4
        outs += [(row, (1, width), F32)] * 2
        scratch = [pltpu.VMEM((ROWS, width), F32)]
    else:
        outs += [(item_block(caption_shape), caption_shape, BF16)]
    return pl.pallas_call(
        partial(attend_backward_kernel, plan, len(arrays), first is not None),
        grid_spec=pltpu.PrefetchScalarGridSpec(
            num_scalar_prefetch=1,
            grid=(items,),
            in_specs=[ANYWHERE] * len(arrays) + specs,
            out_specs=[spec for spec, _, _ in outs],
            scratch_shapes=blocks_scratch(4, width)
            + [
                pltpu.VMEM((width, items * ROWS), BF16),
                pltpu.VMEM((width, items * ROWS), BF16),
                pltpu.VMEM((items * ROWS, width), BF16),
                pltpu.VMEM((items * ROWS, 3 * width), BF16),
                pltpu.VMEM((ROWS, width), BF16),
            ]
            + scratch,
        ),
        out_shape=[jax.ShapeDtypeStruct(shape, kind) for _, shape, kind in outs],
        compiler_params=pltpu.CompilerParams(vmem_limit_bytes=VMEM_BYTES),
        cost_estimate=LONG,
        name="attend_backward",
    )(info, *arrays, *operands)


def normal_parts(u):
    t = pl.reciprocal(1.0 + 0.23164190 * jnp.abs(u), approx=True)
    bell = jnp.exp2((u * -0.7213475204444817) * u)
    poly = t * (
        0.127414796
        + t * (-0.142248368 + t * (0.7107068705 + t * (-0.7265760135 + t * 0.5307027145)))
    )
    tail = poly * bell
    return jnp.where(u < 0, tail, 1.0 - tail), bell


def inner_forward(normed, matrix, bias):
    inner = dot_plain(normed, matrix) + bias
    cumulative, bell = normal_parts(inner)
    slope = cumulative + (inner * 0.3989422804014327) * bell
    return (inner * cumulative).astype(BF16), slope.astype(BF16)


def expert_forward_kernel(plan, weight_count, count, kind, info, *refs):
    weights, refs = refs[:weight_count], refs[weight_count:]
    x_ref, gain_ref, shift_ref, inner_ref, outer_ref = refs[:5]
    y_ref, act_ref, slope_ref, blocks, sems, normed, total = refs[5:]
    step = pl.program_id(0)
    items, _, width = x_ref.shape

    @pl.when(step == 0)
    def _():
        start_weights(info, items, weights, plan, blocks, sems)
        for item in range(items):
            x = x_ref[item, :count].astype(BF16).astype(F32)
            unit, _ = norm_parts(x)
            normed[item * count : (item + 1) * count] = (
                unit * gain_ref[...] + shift_ref[...]
            ).astype(BF16)

    wait_block(blocks, step, sems)
    wait_block(blocks, step + 4, sems)
    for at in range(0, width, 256):
        columns = slice(at, at + 256)
        act, slope = inner_forward(normed[...], blocks[step, :, columns], inner_ref[:, columns])
        act_ref[:, columns] = act
        slope_ref[:, columns] = slope
    part = dot_plain(act_ref[...], blocks[step + 4])

    @pl.when(step == 0)
    def _():
        total[...] = part

    @pl.when(step > 0)
    def _():
        total[...] += part

    @pl.when(step == pl.num_programs(0) - 1)
    def _():
        for item in range(items):
            row_true = true_positions(info[item], 0, count, 0, kind)
            branch = total[item * count : (item + 1) * count] + outer_ref[...]
            x = x_ref[item, :count].astype(BF16).astype(F32)
            y_ref[item, :count] = (x + jnp.where(row_true, branch, 0.0)).astype(BF16)
            if count < ROWS:
                y_ref[item, count:] = jnp.zeros((ROWS - count, width), BF16)


def expert_backward_kernel(plan, weight_count, count, kind, info, *refs):
    weights, refs = refs[:weight_count], refs[weight_count:]
    x_ref, gain_ref, shift_ref, act_ref, slope_ref, grad_ref = refs[:6]
    out_ref, gain_grad_ref, shift_grad_ref, inner_grad_ref, outer_grad_ref = refs[6:11]
    travel_refs = refs[11:15]
    blocks, sems, normed_turned, branch_turned, branch, inner_all, total = refs[15:]
    step = pl.program_id(0)
    items, _, width = x_ref.shape
    section, core = info[items], info[items + 1]

    @pl.when(step == 0)
    def _():
        start_weights(info, items, weights, plan, blocks, sems)
        outer = None
        for item in range(items):
            here = slice(item * count, (item + 1) * count)
            unit, _ = norm_parts(x_ref[item, :count].astype(BF16).astype(F32))
            normed = (unit * gain_ref[...] + shift_ref[...]).astype(BF16)
            row_true = true_positions(info[item], 0, count, 0, kind)
            incoming = grad_ref[item, :count].astype(F32)
            masked = jnp.where(row_true, incoming, 0.0).astype(BF16)
            branch[here] = masked
            store_turned(normed_turned, normed.T, here, section, core)
            store_turned(branch_turned, masked.T, here, section, core)
            term = column_sum(masked)
            outer = term if outer is None else outer + term
        outer_grad_ref[...] = outer

    wait_block(blocks, step, sems)
    wait_block(blocks, step + 4, sems)
    for at in range(0, width, 256):
        columns = slice(at, at + 256)
        act_grad = dot_last(branch[...], blocks[step + 4, columns])
        inner = (slope_ref[:, columns].astype(F32) * act_grad).astype(BF16)
        inner_all[:, columns] = inner
        inner_grad_ref[:, columns] = column_sum(inner)
        put_travel(travel_refs, 0, columns, normed_turned, inner)
        put_travel(travel_refs, 1, columns, branch_turned, act_ref[:, columns])
    part = dot_last(inner_all[...], blocks[step])

    @pl.when(step == 0)
    def _():
        total[...] = part

    @pl.when(step > 0)
    def _():
        total[...] += part

    @pl.when(step == pl.num_programs(0) - 1)
    def _():
        gain_sum, shift_sum = None, None
        for item in range(items):
            unit, scale = norm_parts(x_ref[item, :count].astype(BF16).astype(F32))
            normed_grad = total[item * count : (item + 1) * count]
            gain_part = jnp.sum(normed_grad * unit, axis=0, keepdims=True)
            shift_part = jnp.sum(normed_grad, axis=0, keepdims=True)
            gain_sum = gain_part if gain_sum is None else gain_sum + gain_part
            shift_sum = shift_part if shift_sum is None else shift_sum + shift_part
            incoming = grad_ref[item, :count].astype(F32)
            hidden = incoming + norm_back(normed_grad, unit, scale, gain_ref[...])
            out_ref[item, :count] = hidden.astype(BF16)
            if count < ROWS:
                out_ref[item, count:] = grad_ref[item, count:]
        gain_grad_ref[...] = gain_sum
        shift_grad_ref[...] = shift_sum


def shared_forward_kernel(*refs):
    *rows_refs, inputs_ref, inner_ref, outputs_ref = refs[:7]
    *part_refs, normed, total = refs[7:]
    count = rows_refs[0].shape[0]
    step = pl.program_id(0)

    @pl.when(step == 0)
    def _():
        for index, ref in enumerate(rows_refs):
            normed[index * count : (index + 1) * count] = ref[...]
        total[...] = jnp.zeros_like(total)

    act, _ = inner_forward(normed[...], inputs_ref[...], inner_ref[...])
    total[...] += dot_plain(act, outputs_ref[...])

    @pl.when(step == pl.num_programs(0) - 1)
    def _():
        for index, ref in enumerate(part_refs):
            ref[...] = total[index * count : (index + 1) * count].astype(BF16)


def shared_backward_kernel(plan, weight_count, info, *refs):
    weights, refs = refs[:weight_count], refs[weight_count:]
    rows_refs, grad_refs, inner_ref = refs[:4], refs[4:8], refs[8]
    part_refs, (keep_ref, send_ref, inner_grad_ref, outer_grad_ref) = refs[9:13], refs[13:17]
    blocks, sems, normed, branch, matrix = refs[17:]
    count, width = rows_refs[0].shape
    half = width // 2
    first = info.shape[0] - 3
    core = info[first + 1]
    start_weights(info, first, weights, plan, blocks, sems)
    for index in range(SECTIONS):
        here = slice(index * count, (index + 1) * count)
        normed[here] = rows_refs[index][...]
        branch[here] = grad_refs[index][...]
    outer_grad_ref[...] = column_sum(grad_refs[0][...])
    wait_block(blocks, 0, sems)
    wait_block(blocks, 1, sems)
    part = None
    for at in range(0, width, 256):
        columns = slice(at, at + 256)
        act, slope = inner_forward(normed[...], blocks[0, :, columns], inner_ref[:, columns])
        act_grad = dot_last(branch[...], blocks[1, columns])
        inner = (slope.astype(F32) * act_grad).astype(BF16)
        inner_grad_ref[:, columns] = column_sum(inner)
        matrix[0, :, columns] = dot_first(normed[...], inner).astype(BF16)
        matrix[1, :, columns] = dot_first(branch[...], act).astype(BF16)
        term = dot_last(inner, blocks[0, :, columns])
        part = term if part is None else part + term
    for index, ref in enumerate(part_refs):
        ref[...] = part[index * count : (index + 1) * count].astype(BF16)
    quarter = half // 4
    for which in range(2):
        for group in range(4):
            columns = slice(group * width, (group + 1) * width)
            mine = pl.multiple_of(core * half, 16) + group * quarter
            other = pl.multiple_of((1 - core) * half, 16) + group * quarter
            keep_ref[which, :, columns] = matrix[which, pl.ds(pl.multiple_of(mine, 16), quarter)]
            send_ref[which, :, columns] = matrix[which, pl.ds(pl.multiple_of(other, 16), quarter)]


def chunk_columns(rows, width):
    return pl.BlockSpec((rows, width), lambda step, info: (0, step))


def expert_forward(x, info, weights, gain, shift, inner, outer, count, kind):
    arrays, plan = weights
    items, _, width = x.shape
    hidden = inner.shape[1]
    row = whole_block((1, width))
    return pl.pallas_call(
        partial(expert_forward_kernel, plan, len(arrays), count, kind),
        grid_spec=pltpu.PrefetchScalarGridSpec(
            num_scalar_prefetch=1,
            grid=(hidden // width,),
            in_specs=[ANYWHERE] * len(arrays)
            + [whole_block(x.shape), row, row, chunk_columns(1, width), row],
            out_specs=[
                whole_block((items, ROWS, width)),
                chunk_columns(items * count, width),
                chunk_columns(items * count, width),
            ],
            scratch_shapes=blocks_scratch(8, width)
            + [
                pltpu.VMEM((items * count, width), BF16),
                pltpu.VMEM((items * count, width), F32),
            ],
        ),
        out_shape=[
            jax.ShapeDtypeStruct((items, ROWS, width), BF16),
            jax.ShapeDtypeStruct((items * count, hidden), BF16),
            jax.ShapeDtypeStruct((items * count, hidden), BF16),
        ],
        compiler_params=pltpu.CompilerParams(vmem_limit_bytes=VMEM_BYTES),
        cost_estimate=SHORT,
        name="expert_forward_" + kind,
    )(info, *arrays, x, gain, shift, inner, outer)


def expert_backward(x, info, weights, gain, shift, act, slope, incoming, count, kind):
    arrays, plan = weights
    items, _, width = x.shape
    half = width // 2
    hidden = act.shape[1]
    row = whole_block((1, width))
    travel = pl.BlockSpec((2, half // 2, width), lambda step, info: (0, 0, step))
    return pl.pallas_call(
        partial(expert_backward_kernel, plan, len(arrays), count, kind),
        grid_spec=pltpu.PrefetchScalarGridSpec(
            num_scalar_prefetch=1,
            grid=(hidden // width,),
            in_specs=[ANYWHERE] * len(arrays)
            + [
                whole_block(x.shape),
                row,
                row,
                chunk_columns(items * count, width),
                chunk_columns(items * count, width),
                whole_block(incoming.shape),
            ],
            out_specs=[whole_block(incoming.shape), row, row, chunk_columns(1, width), row]
            + [travel] * 4,
            scratch_shapes=blocks_scratch(8, width)
            + [
                pltpu.VMEM((width, items * count), BF16),
                pltpu.VMEM((width, items * count), BF16),
                pltpu.VMEM((items * count, width), BF16),
                pltpu.VMEM((items * count, width), BF16),
                pltpu.VMEM((items * count, width), F32),
            ],
        ),
        out_shape=[
            jax.ShapeDtypeStruct(incoming.shape, BF16),
            jax.ShapeDtypeStruct((1, width), F32),
            jax.ShapeDtypeStruct((1, width), F32),
            jax.ShapeDtypeStruct((1, hidden), F32),
            jax.ShapeDtypeStruct((1, width), F32),
        ]
        + [jax.ShapeDtypeStruct((2, half // 2, hidden), BF16)] * 4,
        compiler_params=pltpu.CompilerParams(vmem_limit_bytes=VMEM_BYTES),
        cost_estimate=SHORT,
        name="expert_backward_" + kind,
    )(info, *arrays, x, gain, shift, act, slope, incoming)


IN_VMEM = pl.BlockSpec(memory_space=pltpu.VMEM)
IN_SMEM = pl.BlockSpec(memory_space=pltpu.SMEM)


def shared_forward(rows, inputs, inner, outputs):
    count, width = rows[0].shape
    total = SECTIONS * count
    hidden = inner.shape[1]
    return pl.pallas_call(
        shared_forward_kernel,
        grid=(hidden // width,),
        in_specs=[pl.BlockSpec(rows[0].shape, lambda step: (0, 0))] * 4
        + [
            pl.BlockSpec((width, width), lambda step: (0, step)),
            pl.BlockSpec((1, width), lambda step: (0, step)),
            pl.BlockSpec((width, width), lambda step: (step, 0)),
        ],
        out_specs=[pl.BlockSpec((count, width), lambda step: (0, 0))] * SECTIONS,
        scratch_shapes=[pltpu.VMEM((total, width), BF16), pltpu.VMEM((total, width), F32)],
        out_shape=[jax.ShapeDtypeStruct((count, width), BF16)] * SECTIONS,
        compiler_params=pltpu.CompilerParams(vmem_limit_bytes=VMEM_BYTES),
        cost_estimate=SHORT,
        name="shared_forward",
    )(*rows, inputs, inner, outputs)


def shared_backward(rows, grads, info, weights, inner):
    arrays, plan = weights
    count, width = rows[0].shape
    total = SECTIONS * count
    travel = (2, width // 8, 4 * width)
    return pl.pallas_call(
        partial(shared_backward_kernel, plan, len(arrays)),
        in_specs=[IN_SMEM] + [ANYWHERE] * len(arrays) + [IN_VMEM] * 9,
        out_specs=[IN_VMEM] * 8,
        scratch_shapes=blocks_scratch(2, width)
        + [
            pltpu.VMEM((total, width), BF16),
            pltpu.VMEM((total, width), BF16),
            pltpu.VMEM((2, width, width), BF16),
        ],
        out_shape=[
            *[jax.ShapeDtypeStruct((count, width), BF16)] * SECTIONS,
            jax.ShapeDtypeStruct(travel, BF16),
            jax.ShapeDtypeStruct(travel, BF16),
            jax.ShapeDtypeStruct((1, width), F32),
            jax.ShapeDtypeStruct((1, width), F32),
        ],
        compiler_params=pltpu.CompilerParams(vmem_limit_bytes=VMEM_BYTES),
        cost_estimate=SHORT,
        name="shared_backward",
    )(info, *arrays, *rows, *grads, inner)


def plane_turn(plane, planes):
    return ((plane & 1) << 1) | (plane >> 1) if planes == 4 else 0


def finish_kernel(planes, info, scale_ref, *refs):
    step = pl.program_id(0)
    mine, theirs, outs, placed = refs[:4], refs[4:8], refs[8:-1], refs[-1]
    count = mine[0].shape[0]
    width = placed.shape[1]
    half = width // 2
    at = info.shape[0] - 3
    section, core = info[at], info[at + 1]
    turn = plane_turn(info[at + 2], planes)
    turned = turn if count == 1 else jnp.where(section == 1, turn, 0)
    scale = scale_ref[0, 0]
    columns = pl.ds(pl.multiple_of((step ^ turned) * width, width), width)

    def place(which):
        def by_rows():
            for side, pieces in enumerate((mine, theirs)):
                for away, ref in enumerate(pieces):
                    for path in range(2):
                        row = (core ^ side) * half + path * (half // 2)
                        row = row + (section ^ away) * PIECE_ROWS
                        placed[pl.ds(pl.multiple_of(row, 16), PIECE_ROWS), :] = ref[
                            which, path * PIECE_ROWS : (path + 1) * PIECE_ROWS, columns
                        ].astype(F32)

        def by_columns():
            for side, pieces in enumerate((mine, theirs)):
                for away, ref in enumerate(pieces):

                    @pl.when(step == away)
                    def _(side=side, ref=ref):
                        for group in range(4):
                            quarter = half // 4
                            row = (core ^ side) * half + group * quarter
                            placed[pl.ds(pl.multiple_of(row, 16), quarter), :] = ref[
                                which, :, group * width : (group + 1) * width
                            ].astype(F32)

        if count == 1:
            by_rows()
        else:
            pl.when(section != 0)(by_rows)
            pl.when(section == 0)(by_columns)

    place(0)
    if count == 1:

        @pl.when(step < 3)
        def _():
            outs[0][0] = placed[...] / scale

        @pl.when(step == 3)
        def _():
            outs[1][0] = placed[...] / scale

    else:
        outs[0][0] = placed[...] / scale
        place(1)
        outs[1][0] = (placed[...] / scale).T


def finish(info, scale, mine, theirs, planes):
    count, _, hidden = mine[0].shape
    width = hidden // 4
    if count == 1:
        shapes = [(1, width, 3 * width), (1, width, width)]
        maps = [lambda step, info: (0, 0, jnp.minimum(step, 2)), lambda step, info: (0, 0, 0)]
    else:
        shapes = [(1, width, hidden), (1, hidden, width)]
        maps = [lambda step, info: (0, 0, step), lambda step, info: (0, step, 0)]
    return pl.pallas_call(
        partial(finish_kernel, planes),
        grid_spec=pltpu.PrefetchScalarGridSpec(
            num_scalar_prefetch=1,
            grid=(4,),
            in_specs=[IN_SMEM] + [whole_block(mine[0].shape)] * 8,
            out_specs=[pl.BlockSpec((1, width, width), at) for at in maps],
            scratch_shapes=[pltpu.VMEM((width, width), F32)],
        ),
        out_shape=[jax.ShapeDtypeStruct(shape, F32) for shape in shapes],
        compiler_params=pltpu.CompilerParams(vmem_limit_bytes=VMEM_BYTES),
        cost_estimate=SHORT,
        name="finish",
    )(info, scale, *mine, *theirs)


def pack_kernel(count, plan, info, *refs):
    sources, outs, sems = refs[:count], refs[count:-1], refs[-1]
    first = info.shape[0] - 3
    section, core, plane = info[first], info[first + 1], info[first + 2]
    half = outs[0].shape[1]
    for index, (out, choices) in enumerate(zip(outs, plan)):
        for at, at_plane, parts in choices:
            here = section == at
            if at_plane is not None:
                here = here & (plane == at_plane)

            @pl.when(here)
            def _(index=index, out=out, parts=parts):
                for block, part in enumerate(parts):
                    if part[0] == "own":
                        _, which, row, column = part
                        rows = pl.ds(pl.multiple_of(row + core * half, half), half)
                        source = sources[which].at[rows, pl.ds(column, out.shape[2])]
                    else:
                        source = sources[part[1]].at[block]
                    pltpu.make_async_copy(source, out.at[block], sems.at[index, block]).start()

    for index, out in enumerate(outs):
        for block in range(2):
            pltpu.make_async_copy(out.at[block], out.at[block], sems.at[index, block]).wait()


def pack(info, sources, plan, shape):
    return pl.pallas_call(
        partial(pack_kernel, len(sources), plan),
        in_specs=[IN_SMEM] + [ANYWHERE] * len(sources),
        out_specs=[IN_VMEM] * len(plan),
        scratch_shapes=[pltpu.SemaphoreType.DMA((len(plan), 2))],
        out_shape=[jax.ShapeDtypeStruct(shape, BF16)] * len(plan),
        cost_estimate=SHORT,
        name="pack",
    )(info, *sources)


def over_section(value, bits, sources=range(SECTIONS)):
    return lax.ppermute(value, "section", [(at, at ^ bits) for at in sources])


def over_core(value):
    return lax.ppermute(value, "core", [(0, 1), (1, 0)])


def over_plane(value, pairs):
    return lax.ppermute(value, "z", pairs)


def added(left, right):
    return (left.astype(F32) + right.astype(F32)).astype(BF16)


def after(value, *earlier):
    return lax.optimization_barrier((value,) + earlier)[0]


def under(outputs, *arrivals):
    joined = lax.optimization_barrier(tuple(outputs) + arrivals)
    return list(joined[: len(outputs)]), list(joined[len(outputs) :])


def by_section(section, values):
    result, last = None, None
    for at in sorted(values):
        if result is None:
            result = values[at]
        elif values[at] is not last:
            result = jnp.where(section >= at, values[at], result)
        last = values[at]
    return result


def total(*values):
    result = values[0].astype(F32)
    for value in values[1:]:
        result = result + value.astype(F32)
    return result.astype(BF16)


class Sums:
    def __init__(self, travel):
        self.stay, self.move, self.other_stay, self.other_move = travel
        self.size = self.stay.shape[1] // 2

    def cross(self, *earlier):
        if earlier:
            self.other_move = after(self.other_move, *earlier)
            self.other_stay = after(self.other_stay, *earlier)
        self.got_move, self.got_stay = over_core(self.other_move), over_core(self.other_stay)

    def first_sends(self):
        size = self.size
        self.sent = [
            total(self.move[:, at : at + size], self.got_move[:, at : at + size])
            for at in (0, size)
        ]
        return self.sent

    def second_sends(self, from_x, from_y):
        size, half = self.size, self.size // 2
        self.first = from_x, from_y
        to_y = total(self.stay[:, half:size], self.got_stay[:, half:size], from_x[:, half:])
        to_x = total(
            self.stay[:, size + half :], self.got_stay[:, size + half :], from_y[:, half:]
        )
        self.sent = [to_x, to_y]
        return self.sent

    def whole(self, from_x, from_y):
        size, half = self.size, self.size // 2
        parts = []
        for at, first, second in ((0, self.first[0], from_y), (size, self.first[1], from_x)):
            here = slice(at, at + half)
            parts.append(total(self.stay[:, here], self.got_stay[:, here], first[:, :half], second))
        return jnp.concatenate(parts, axis=1)


def over_links(sends):
    return [over_section(sends[0], 1), over_section(sends[1], 2)]


class Planes:
    def __init__(self, value, plane, planes):
        self.value, self.plane, self.planes, self.turn = value, plane, planes, 0

    def sends(self, *earlier):
        value = after(self.value, *earlier) if earlier else self.value
        if self.planes != 4:
            return (value,)
        bits = (1, 2, 2, 1)[self.turn]
        if self.turn < 2:
            bit = (self.plane & 1, self.plane >> 1)[self.turn]
            size = value.shape[-1] // 2
            value = lax.dynamic_slice_in_dim(value, (1 - bit) * size, size, value.ndim - 1)
        return (over_plane(value, [(at, at ^ bits) for at in range(4)]),)

    def take(self, arrived):
        if self.planes != 4:
            self.value = lax.psum(arrived, "z") if self.turn == 3 else arrived
        elif self.turn < 2:
            bit = (self.plane & 1, self.plane >> 1)[self.turn]
            size = self.value.shape[-1] // 2
            keep = lax.dynamic_slice_in_dim(self.value, bit * size, size, self.value.ndim - 1)
            self.value = added(keep, arrived)
        else:
            self.value = jnp.concatenate([self.value, arrived], axis=-1)
        self.turn += 1

    def in_order(self, value):
        if self.planes != 4:
            return value
        size, turn = value.shape[-1] // 4, plane_turn(self.plane, 4)
        parts = [
            lax.dynamic_slice_in_dim(value, (at ^ turn) * size, size, value.ndim - 1)
            for at in range(4)
        ]
        return jnp.concatenate(parts, axis=-1)


class Weights:
    def __init__(self, own, info, planes):
        self.own, self.info = own, info
        self.four = planes == 4
        self.plan = PLAN_FOUR if self.four else PLAN_ANY
        self.half, self.width = own[1].shape[0] // 2, own[1].shape[1]
        self.mine, self.theirs, self.arrived = {}, {}, {}

    def place(self, layer, block):
        if layer in "ac":
            return (0, 0, block * self.width) if block < 3 else (1, 0, 0)
        if layer == "g":
            return (2, 0, block * self.width) if block < 4 else (3, (block - 4) * self.width, 0)
        return (2, 0, block * self.width) if block < 4 else (3, (block - 4) * self.width, 0)

    def choices(self, sends, sources):
        result = []
        for at in range(SECTIONS):
            name = sends.get(at)
            if name is not None and HOMES[name[0]] != at:
                key = self.arrived[at, name]
                if key not in sources:
                    sources[key] = len(self.own) + len(sources)
                result.append((at, None, [("arrived", sources[key])] * 2))
                continue
            for plane in range(4) if name == "F" else (None,):
                piece = ("f" + str(plane)) if name == "F" else name or "a0"
                layer, index = piece[0], int(piece[1])
                if layer in "ac":
                    blocks = ATTEND_BLOCKS[index]
                else:
                    blocks = (index, 4 + index) if layer == "g" else EXPERT_BLOCKS[index]
                parts = [("own",) + self.place(layer, block) for block in blocks]
                result.append((at, plane, parts))
        return result

    def packed(self, wanted):
        sources = {}
        plan = [self.choices(sends, sources) for sends in wanted]
        arrays = list(self.own) + [self.mine[key] for key in sources]
        return pack(self.info, arrays, plan, (2, self.half, self.width))

    def sends(self, step):
        if step == "F":
            return [{at: "F" for at in range(SECTIONS)}]
        return [sends for sends in self.plan[step] if sends]

    def payloads(self, *steps):
        wanted = [sends for step in steps for sends in self.sends(step)]
        return list(self.packed(wanted))

    def move(self, step, payloads):
        links = [(link, sends) for link, sends in enumerate(self.plan[step]) if sends]
        for (link, sends), payload in zip(links, payloads):
            self.mine[step, link] = over_section(payload, link + 1, sorted(sends))
            for at, name in sends.items():
                self.arrived[at ^ (link + 1), name] = (step, link)
        return [(step, link) for link, _ in links]

    def move_planes(self, step):
        up, down = self.mine["plane", step - 1], self.mine["plane", 1 - step]
        up = over_plane(up, [(at, at + 1) for at in range(step - 1, 3)])
        down = over_plane(down, [(at, at - 1) for at in range(4 - step, 0, -1)])
        self.mine["plane", step], self.mine["plane", -step] = up, down
        return [("plane", step), ("plane", -step)]

    def cross(self, keys):
        for key in keys:
            self.theirs[key] = over_core(self.mine[key])
        return keys

    def join(self, outputs, mine=(), theirs=()):
        values = [self.mine[key] for key in mine] + [self.theirs[key] for key in theirs]
        outputs, values = under(outputs, *values)
        for key, value in zip(mine, values):
            self.mine[key] = value
        for key, value in zip(theirs, values[len(mine) :]):
            self.theirs[key] = value
        return outputs

    def layer(self, layer):
        arrays, places = list(self.own), {}

        def place(key):
            if key not in places:
                places[key] = len(arrays)
                arrays.extend([self.mine[key], self.theirs[key]])
            return places[key], places[key] + 1

        if layer in "ac":
            names = [(layer + str(index), ATTEND_BLOCKS[index]) for index in range(2)]
        else:
            names = [(layer + str(index), EXPERT_BLOCKS[index]) for index in range(4)]
        plan = []
        for at in range(SECTIONS):
            if layer == "g":
                names = [("g" + str(at), (0, 1))]
            if HOMES[layer] == at:
                steps = []
                for name, blocks in names:
                    for block in blocks:
                        source = block * 4 if layer == "g" else block
                        steps.append((block, ("own",) + self.place(layer, source)))
                plan.append((at, None, steps))
                continue
            by_plane = layer == "f" and self.four
            for plane in range(4) if by_plane else (None,):
                steps = []
                for index, (name, blocks) in enumerate(names):
                    key = ("plane", plane - index) if by_plane else self.arrived[at, name]
                    for which, block in enumerate(blocks):
                        steps.append((block, ("piece",) + place(key) + (which,)))
                plan.append((at, plane, steps))
        return arrays, plan


def per_device(
    tokens,
    caption_lengths,
    attend_gain,
    attend_shift,
    attend_inputs,
    attend_bias,
    attend_output,
    expert_gain,
    expert_shift,
    expert_inputs,
    expert_inner_bias,
    expert_outputs,
    expert_outer_bias,
    cotangent,
):
    section, core, plane = lax.axis_index("section"), lax.axis_index("core"), lax.axis_index("z")
    planes = lax.axis_size("z")
    items, positions, width = tokens.shape
    hidden = expert_inputs.shape[-1]
    info = [value.reshape(1).astype(jnp.int32) for value in (section, core, plane)]
    info = jnp.concatenate([caption_lengths] + info)
    weights = Weights(
        (attend_inputs[0], attend_output[0], expert_inputs[0], expert_outputs[0]), info, planes
    )

    def to_sections(value):
        return [value] + [over_section(value, bits) for bits in (1, 2, 3)]

    def items_of(part):
        return part.reshape(items, CAP_ROWS, width)

    keys = weights.move(0, weights.payloads(0))
    pad = ((0, 0), (0, ROWS - positions), (0, 0))
    x0 = jnp.pad(tokens, pad)
    last_grad = jnp.pad(cotangent, pad)
    rows = jnp.concatenate(
        [
            attend_gain,
            attend_shift,
            attend_bias,
            expert_gain,
            expert_shift,
            expert_inner_bias,
            expert_outer_bias,
            jnp.full((1, 128), jnp.sum(caption_lengths), F32),
        ],
        axis=1,
    )
    rows = to_sections(rows)
    x0, last_grad, *rows = weights.join([x0, last_grad, *rows], keys)
    keys1 = weights.move(1, weights.payloads(1))
    rows = jnp.concatenate(rows, axis=0)
    language_count = jnp.sum(rows[:, -128:], axis=0, keepdims=True)
    rows = [lax.dynamic_index_in_dim(rows, at ^ section, 0) for at in range(SECTIONS)]
    sizes = [width, width, 3 * width, width, width, hidden, width]
    ends = [sum(sizes[: at + 1]) for at in range(len(sizes))]
    used = [(0, 0), (0, 1), (0, 2), (0, 3), (0, 4), (0, 5), (1, 3), (1, 4), (1, 5), (1, 6)]
    used += [(0, 6), (2, 0), (2, 1), (2, 2), (3, 3), (3, 4), (3, 5), (3, 6)]
    kept = [rows[slot][:, ends[which] - sizes[which] : ends[which]] for slot, which in used]
    language_count, *kept = weights.join([language_count, *kept], keys1)
    kept = dict(zip(used, kept))

    def row(slot, which):
        return kept[slot, which]

    crossed = weights.cross(keys + keys1)
    sends = weights.payloads(2, "F") if weights.four else weights.payloads(2)
    sends, (info, language_count) = under(sends, info, language_count)
    keys = weights.move(2, sends[:2])
    info, language_count = weights.join(
        [info, language_count + over_core(language_count)], theirs=crossed
    )
    plane_keys = []
    if weights.four:
        weights.mine["plane", 0] = sends[2]
        plane_keys = weights.move_planes(1)
    attend0 = weights.layer("a")
    outputs = attend_forward(
        x0, info, attend0, row(0, 0), row(0, 1), row(0, 2), following=(row(0, 3), row(0, 4))
    )
    y0, qkv0, mixed0, caption_rows = weights.join(outputs, keys)
    caption_rows = to_sections(caption_rows.reshape(-1, width))
    sends = weights.payloads(3, 4) if weights.four else weights.payloads(3)
    caption_rows = weights.join(caption_rows, plane_keys)
    sends, caption_rows = under(sends, *caption_rows)
    early_keys = keys
    keys, sends = weights.move(3, sends[:2]), sends[2:]
    crossed = weights.cross(early_keys)
    if weights.four:
        keys += weights.move_planes(2)
    outputs = shared_forward(caption_rows, expert_inputs[0], expert_inner_bias, expert_outputs[0])
    part = weights.join(outputs, keys, crossed)
    (y0,) = weights.join([y0], theirs=weights.cross([(3, 0), (3, 1)]))
    branch = {at: over_section(part[at], at, [0]) for at in range(1, SECTIONS)}
    keys = weights.move_planes(3) if weights.four else []
    expert1 = weights.layer("e")
    outputs = expert_forward(
        y0, info, expert1, row(1, 3), row(1, 4), row(1, 5), row(1, 6), PATCH_ROWS, "patch"
    )
    outputs, moved = under(outputs, *branch.values())
    if weights.four:
        keys += [("plane", step) for step in range(-2, 3)]
    x2, act1, slope1 = weights.join(outputs, keys)
    branch = dict(zip(branch, moved))
    branch[0] = part[0]
    branch = items_of(by_section(section, branch))
    if weights.four:
        crossed = [("plane", step) for step in range(-3, 4)]
    else:
        for step in (4, 5):
            weights.move(step, weights.payloads(step))
        crossed = [(4, 0), (4, 1), (5, 0)]
    weights.cross(crossed)
    attend2 = weights.layer("c") if weights.four else None
    if not weights.four:
        (x2,) = weights.join([x2], theirs=crossed)
        attend2 = weights.layer("c")
    outputs = attend_forward(
        x2, info, attend2, row(2, 0), row(2, 1), row(2, 2), merge=(y0, branch, row(0, 6))
    )
    if weights.four:
        language_count += over_plane(language_count, [(at, at ^ 1) for at in range(4)])
    x3, qkv2, mixed2, x2, language_count = weights.join([*outputs, language_count], theirs=crossed)
    if weights.four:
        language_count += over_plane(language_count, [(at, at ^ 2) for at in range(4)])
    else:
        language_count = lax.psum(language_count, "z")
    expert3 = weights.layer("f")
    outputs = expert_forward(
        x3, info, expert3, row(3, 3), row(3, 4), row(3, 5), row(3, 6), ROWS, "all"
    )
    layer_output, act3, slope3, language_count = under([*outputs, language_count])[0]
    language_count = language_count[0, 0].astype(jnp.int32)
    vision_count = PATCHES * items * SECTIONS * 2 * planes
    counts = jnp.stack(
        [jnp.full((), vision_count, jnp.int32), language_count, language_count + vision_count]
    )

    def small_rows(values):
        flat = jnp.concatenate(values, axis=1)
        count = -(-flat.shape[1] // hidden)
        flat = jnp.pad(flat, ((0, 0), (0, count * hidden - flat.shape[1])))
        return flat.reshape(count, hidden)

    def to_home(sums, diagonal_last=False):
        got = [by_section(section, sums)]
        for bits in (1, 2, 3):
            sends = {at ^ bits: sums[at] for at in sums}
            payload = by_section(section, sends)
            if bits == 3 and diagonal_last:
                payload = after(payload, got[2])
            got.append(over_section(payload, bits, sorted(sends)))
        return got

    keys = []
    if weights.four:
        sends, (layer_output, last_grad) = under(sends, layer_output, last_grad)
        keys = weights.move(4, sends)
    outputs = expert_backward(
        x3, info, expert3, row(3, 3), row(3, 4), act3, slope3, last_grad, ROWS, "all"
    )
    outputs = weights.join(outputs, keys)
    crossed = weights.cross(keys)
    grad3, *small3 = outputs[:5]
    sums3 = Sums(outputs[5:])
    sums3.cross()
    moved = over_links(sums3.first_sends())
    grad3 = after(grad3, *sums3.sent)
    outputs = attend_backward(
        x2, info, attend2, row(2, 0), row(2, 1), qkv2, mixed2, grad3
    )
    outputs, moved = under(outputs, *moved, sums3.got_stay)
    outputs = weights.join(outputs, theirs=crossed)
    grad2, *small2 = outputs[:4]
    sums2, caption_grad = Sums(outputs[4:8]), outputs[8]
    caption_grads = to_sections(caption_grad.reshape(-1, width))
    sums3.got_stay = moved[2]
    moved3 = over_links(sums3.second_sends(*moved[:2]))
    grad2 = after(grad2, *sums3.sent)
    outputs = expert_backward(
        y0, info, expert1, row(1, 3), row(1, 4), act1, slope1, grad2, PATCH_ROWS, "patch"
    )
    outputs, caption_grads = under(outputs, *caption_grads)
    grad1, *small1 = outputs[:5]
    sums2.cross(grad1)
    sums1 = Sums(outputs[5:])
    sums1.cross()
    inner_quarter = lax.dynamic_slice(row(0, 5), (0, section * width), (1, width))
    sum3 = sums3.whole(*moved3)
    inner_quarter = after(inner_quarter, grad1, sum3)
    outputs = shared_backward(
        caption_rows, caption_grads, info, weights.layer("g"), inner_quarter
    )
    parts, (keep0, send0, inner_grad, outer_grad) = outputs[:4], outputs[4:]
    got = [over_section(parts[bits], bits) for bits in (1, 2, 3)]
    sends = [after(value, *parts) for value in sums1.first_sends()]
    moved1 = over_links(sends)
    keep0 = added(keep0, over_core(send0))
    early = lax.psum(jnp.concatenate([sum3, keep0], axis=0), "z")
    sends2 = [after(value, *sends) for value in sums2.first_sends()]
    moved2 = over_links(sends2)
    parts = [parts[0], *got]
    grad1 = after(grad1, keep0, *sends, *sends2)
    outputs = attend_backward(
        x0,
        info,
        attend0,
        row(0, 0),
        row(0, 1),
        qkv0,
        mixed0,
        grad1,
        first=(y0, row(0, 3), parts),
    )
    outputs, moved = under(outputs, *moved2, *moved1)
    moved2, moved1 = moved[:2], moved[2:]
    tokens_grad, *small_first = outputs[:4]
    sums_first, gain_grad, shift_grad = Sums(outputs[4:8]), outputs[8], outputs[9]
    sums_first.cross()
    inner_grad = lax.dynamic_update_slice(
        jnp.zeros((1, hidden), F32), inner_grad, (0, section * width)
    )
    small = small_rows(
        small_first + [gain_grad, shift_grad, inner_grad, outer_grad] + small2 + small1 + small3
    )
    small = added(small, over_core(small))
    to_x, to_y = sums_first.first_sends()
    to_x = jnp.concatenate([to_x[0], small], axis=0)
    sends = lax.optimization_barrier((*sums1.second_sends(*moved1), to_x, to_y))
    moved1, moved = over_links(sends[:2]), over_links(sends[2:])
    sum1, early = lax.optimization_barrier((sums1.whole(*moved1), early))
    planes1 = Planes(sum1, plane, planes)
    size = to_y.shape[1]
    small = added(small, moved[0][size:])
    to_x, to_y = sums_first.second_sends(moved[0][None, :size], moved[1])
    early_x, early_y = sums2.second_sends(*moved2)
    to_x = jnp.concatenate([to_x[0], early_x[0]], axis=0)
    to_y = jnp.concatenate([to_y[0], early_y[0], small], axis=0)
    to_x, to_y = lax.optimization_barrier((to_x, to_y))
    sent1 = planes1.sends()
    moved = lax.optimization_barrier(tuple(over_links((to_x, to_y))))
    size = early_x.shape[1]
    last = sums_first.whole(moved[0][None, :size], moved[1][None, :size])
    sum2 = sums2.whole(moved[0][None, size:], moved[1][None, size : 2 * size])
    small = added(small, moved[1][2 * size :])
    small_count = small.shape[0]
    eighth = last.shape[1]
    last = jnp.concatenate([last[0], sum2[0], small], axis=0)
    planes_last = Planes(last, plane, planes)
    home_early = to_home({0: after(early[2:], *moved), 3: after(early[:2], *moved)}, diagonal_last=True)
    planes_last.take(*planes_last.sends())
    planes1.take(*sent1)
    planes1.take(*planes1.sends())
    planes1.take(*planes1.sends())
    planes1.take(*planes1.sends())
    planes_last.take(*planes_last.sends())
    planes_last.take(*planes_last.sends())
    home_late = to_home({1: after(planes1.value, *home_early[1:3])})
    planes_last.take(*planes_last.sends())
    last = planes_last.value
    home_attend = to_home({0: last[None, :eighth], 2: last[None, eighth : 2 * eighth]})
    small = planes_last.in_order(last[2 * eighth :].astype(F32))

    as_float = counts.astype(F32)
    one = jnp.ones((), F32)
    attend_scales = jnp.stack([as_float[2], one, as_float[2], one])
    expert_scales = jnp.stack([as_float[1], as_float[0], one, as_float[2]])

    def placed(pieces, theirs, scales):
        scale = lax.dynamic_index_in_dim(scales, section, 0).reshape(1, 1)
        return finish(info, scale, pieces, theirs, planes)

    blank = jnp.zeros_like(home_late[0])
    pieces, theirs = [], []
    for early, late in zip(home_early, home_late):
        pieces.append(by_section(section, {0: early, 1: late, 2: blank, 3: early}))
        before = theirs[-1:] + (home_attend[1:3] if len(theirs) == 3 else [])
        theirs.append(over_core(after(pieces[-1], *before) if before else pieces[-1]))
    inputs_whole, outputs_whole = placed(pieces, theirs, expert_scales)
    inputs_whole, home_attend[3] = lax.optimization_barrier((inputs_whole, home_attend[3]))
    blank = jnp.zeros_like(home_attend[0])
    pieces = [by_section(section, {0: got, 1: blank, 2: got, 3: blank}) for got in home_attend]
    theirs = [over_core(piece) for piece in pieces]
    attend_whole, output_whole = placed(pieces, theirs, attend_scales)

    attend_size, expert_size = 5 * width, 3 * width + hidden
    cuts = [attend_size, attend_size + expert_size]
    cuts += [cuts[1] + attend_size, cuts[1] + attend_size + expert_size]
    small = jnp.split(small.reshape(-1)[: cuts[3] + expert_size], cuts)
    none_attend, none_expert = jnp.zeros_like(small[0]), jnp.zeros_like(small[1])
    attend_small = jnp.stack([small[0], none_attend, small[2], none_attend])
    expert_small = jnp.stack([small[1], small[3], none_expert, small[4]])
    attend_small = attend_small / attend_scales.reshape(-1, 1)
    expert_small = expert_small / expert_scales.reshape(-1, 1)
    attend_small = lax.dynamic_index_in_dim(attend_small, section, 0)
    expert_small = lax.dynamic_index_in_dim(expert_small, section, 0)
    return (
        layer_output[:, :positions],
        tokens_grad[:, :positions],
        attend_small[:, :width],
        attend_small[:, width : 2 * width],
        attend_whole,
        attend_small[:, 2 * width :],
        output_whole,
        expert_small[:, :width],
        expert_small[:, width : 2 * width],
        inputs_whole,
        expert_small[:, 2 * width : 2 * width + hidden],
        outputs_whole,
        expert_small[:, 2 * width + hidden :],
        counts,
    )


def solution(mesh):
    sections, groups = mesh.shape["section"], mesh.shape["dp"]
    split = Mesh(mesh.devices.reshape(sections, groups // 2, 2), ("section", "z", "core"))
    items = P(("section", "z", "core"), None, None)
    flat = P("section", None)
    matrix = P("section", None, None)
    placed = (
        items,
        P(("section", "z", "core")),
        flat,
        flat,
        matrix,
        flat,
        matrix,
        flat,
        flat,
        matrix,
        flat,
        matrix,
        flat,
        items,
    )
    return jax.shard_map(
        per_device,
        mesh=split,
        in_specs=placed,
        out_specs=(
            items,
            items,
            flat,
            flat,
            matrix,
            flat,
            matrix,
            flat,
            flat,
            matrix,
            flat,
            matrix,
            flat,
            P(),
        ),
        check_vma=False,
    )
```

profile of v0, /device:TPU:27, one launch (start us, length us, event | category | flops | bytes accessed | tf_op | source)
XLA Modules:
  0.0 646.3 jit_solution(379878989696474649)
XLA Ops:
  8.6 3.8 pack.4
  21.0 19.4 %collective-permute-done = f32[1,9344]{1,0:T(1,128)} collective-permute-done((f32[1,9344]{1,0:T(1,128)S(1)}, f32[1,9344]{1,0:T(1,128)}, u32[]{:S(2)}, u32[]{:S(2)}) %collective-permute-start) | collective-permute-done | bytes 37408 | tf_op jit(solution)/shard_map/ppermute | solution.py:914
  41.9 1.9 collective-permute-start.8
  43.9 3.7 pack.5
  54.0 22.9 %collective-permute-done.5.refs_6_.refs_5_ = bf16[2,384,768]{2,1,0:T(8,128)(2,1)} collective-permute-done((bf16[2,384,768]{2,1,0:T(8,128)(2,1)}, bf16[2,384,768]{2,1,0:T(8,128)(2,1)}, u32[]{:S(2)}, u32[]{:S(2)}) %collective-permute-start.5) | collective-permute-done | bytes 1179680 | tf_op jit(solution)/shard_map/ppermute | solution.py:914
  78.3 4.5 pack.6
  82.8 2.9 collective-permute-start.12
  90.9 5.0 collective-permute-start.18
  95.9 13.9 %attend_forward.2 = (f32[3,256,768]{2,1,0:T(8,128)}, bf16[3,256,2304]{2,1,0:T(8,128)(2,1)}, bf16[3,256,768]{2,1,0:T(8,128)(2,1)}, bf16[3,48,768]{2,1,0:T(8,128)(2,1)}) custom-call(s32[6]{0:T(128)} %pad_add_fusion.info, bf16[768,2304]{1,0:T(8,128)(2,1)} %bitcast.87, bf16[768,768]{1,0:T(8,128)(2,1)} %bitcast.100, bf16[768,3072]{1,0:T(8,128)(2,1)} %bitcast.59, ...), custom_call_target="tpu_custom_call" | custom-call | bytes 100000 | tf_op jit(solution)/shard_map/attend_forward/pallas_call | solution.py:380
  109.8 2.2 collective-permute-done.12.refs_6_.refs_8_.refs_14_
  113.7 2.9 collective-permute-start.14
  118.5 2.2 collective-permute-start.16
  120.7 4.5 pack.7
  129.3 2.4 collective-permute-start.20
  133.8 13.0 %shared_forward.1 = (bf16[144,768]{1,0:T(8,128)(2,1)}, bf16[144,768]{1,0:T(8,128)(2,1)}, bf16[144,768]{1,0:T(8,128)(2,1)}, bf16[144,768]{1,0:T(8,128)(2,1)}) custom-call(bf16[144,768]{1,0:T(8,128)(2,1)} %bitcast.114, bf16[144,768]{1,0:T(8,128)(2,1)} %collective-permute-done.14.refs_1_.refs_9_, bf16[144,768]{1,0:T(8,128)(2,1)} %collective-permute-done.15.refs_2_.refs_10_, ...), custom_call_target="tpu_custom_call" | custom-call | bytes 100000 | tf_op jit(solution)/shard_map/shared_forward/pallas_call | solution.py:739
  146.8 8.6 %collective-permute-done.19.refs_10_.refs_4_ = bf16[2,384,768]{2,1,0:T(8,128)(2,1)S(1)} collective-permute-done((bf16[2,384,768]{2,1,0:T(8,128)(2,1)}, bf16[2,384,768]{2,1,0:T(8,128)(2,1)S(1)}, u32[]{:S(2)}, u32[]{:S(2)}) %collective-permute-start.19) | collective-permute-done | bytes 1179680 | tf_op jit(solution)/shard_map/ppermute | solution.py:914
  157.3 2.4 collective-permute-done.21.refs_14_
  160.8 2.6 collective-permute-start.25
  170.7 19.6 %expert_forward_patch.1 = (bf16[3,256,768]{2,1,0:T(8,128)(2,1)}, bf16[624,3072]{1,0:T(8,128)(2,1)}, bf16[624,3072]{1,0:T(8,128)(2,1)}) custom-call(s32[6]{0:T(128)} %pad_add_fusion.info, bf16[768,2304]{1,0:T(8,128)(2,1)} %bitcast.89, bf16[768,768]{1,0:T(8,128)(2,1)} %bitcast.102, bf16[768,3072]{1,0:T(8,128)(2,1)} %bitcast.62, bf16[3072,768]{1,0:T(8,128)(2,1)} %bitcast.76, ...), custom_call_target="tpu_custom_call" | custom-call | bytes 100000 | tf_op jit(solution)/shard_map/expert_forward_patch/pallas_call | solution.py:656
  190.3 3.1 collective-permute-done.30.refs_16_
  198.6 1.9 collective-permute-done.34.refs_9_
  203.2 13.9 %attend_forward.3 = (bf16[3,256,768]{2,1,0:T(8,128)(2,1)}, bf16[3,256,2304]{2,1,0:T(8,128)(2,1)}, bf16[3,256,768]{2,1,0:T(8,128)(2,1)}, bf16[3,256,768]{2,1,0:T(8,128)(2,1)}) custom-call(s32[6]{0:T(128)} %pad_add_fusion.info, bf16[768,2304]{1,0:T(8,128)(2,1)} %bitcast.90, bf16[768,768]{1,0:T(8,128)(2,1)} %bitcast.103, bf16[768,3072]{1,0:T(8,128)(2,1)} %bitcast.63, ...), custom_call_target="tpu_custom_call" | custom-call | bytes 100000 | tf_op jit(solution)/shard_map/attend_forward/pallas_call | solution.py:380
  217.2 2.1 collective-permute-start.40
  219.3 22.0 %expert_forward_all.1 = (bf16[3,256,768]{2,1,0:T(8,128)(2,1)}, bf16[768,3072]{1,0:T(8,128)(2,1)}, bf16[768,3072]{1,0:T(8,128)(2,1)}) custom-call(s32[6]{0:T(128)} %pad_add_fusion.info, bf16[768,2304]{1,0:T(8,128)(2,1)} %bitcast.91, bf16[768,768]{1,0:T(8,128)(2,1)} %bitcast.104, bf16[768,3072]{1,0:T(8,128)(2,1)} %bitcast.64, bf16[3072,768]{1,0:T(8,128)(2,1)} %bitcast.78, ...), custom_call_target="tpu_custom_call" | custom-call | bytes 100000 | tf_op jit(solution)/shard_map/expert_forward_all/pallas_call | solution.py:656
  241.9 4.2 collective-permute-start.41
  246.1 29.7 %expert_backward_all.1 = (bf16[3,256,768]{2,1,0:T(8,128)(2,1)}, f32[1,768]{1,0:T(1,128)}, f32[1,768]{1,0:T(1,128)}, f32[1,3072]{1,0:T(1,128)}, f32[1,768]{1,0:T(...) custom-call(s32[6]{0:T(128)} %pad_add_fusion.info, ...), custom_call_target="tpu_custom_call" | custom-call | bytes 100000 | tf_op jit(solution)/shard_map/expert_backward_all/pallas_call | solution.py:692
  277.0 3.9 collective-permute-done.42
  280.9 3.9 add_convert_fusion.3
  284.8 2.7 collective-permute-start.43
  287.5 29.4 %attend_backward.2 = (bf16[3,256,768]{2,1,0:T(8,128)(2,1)}, f32[1,768]{1,0:T(1,128)}, f32[1,768]{1,0:T(1,128)}, f32[1,2304]{1,0:T(1,128)}, bf16[1,192,3072]{2,1,...) custom-call(s32[6]{0:T(128)} %pad_add_fusion.info, ...), custom_call_target="tpu_custom_call" | custom-call | flops 30000001024 | bytes 30000000 | tf_op jit(solution)/shard_map/attend_backward/pallas_call | solution.py:432
  319.6 2.7 add_convert_fusion.17
  324.3 27.9 %expert_backward_patch.1 = (bf16[3,256,768]{2,1,0:T(8,128)(2,1)}, f32[1,768]{1,0:T(1,128)}, f32[1,768]{1,0:T(1,128)}, f32[1,3072]{1,0:T(1,128)}, f32[1,768]{1,0:...) custom-call(s32[6]{0:T(128)} %pad_add_fusion.info, ...), custom_call_target="tpu_custom_call" | custom-call | bytes 100000 | tf_op jit(solution)/shard_map/expert_backward_patch/pallas_call | solution.py:692
  353.0 10.0 %shared_backward.1 = (bf16[144,768]{1,0:T(8,128)(2,1)}, bf16[144,768]{1,0:T(8,128)(2,1)}, bf16[144,768]{1,0:T(8,128)(2,1)}, bf16[144,768]{1,0:T(8,128)(2,1)}, bf...) custom-call(s32[6]{0:T(128)} %pad_add_fusion.info, ...), custom_call_target="tpu_custom_call" | custom-call | bytes 100000 | tf_op jit(solution)/shard_map/shared_backward/pallas_call | solution.py:762
  363.0 2.1 collective-permute-start.52
  369.3 3.0 add_convert_fusion.16
  378.0 2.7 add_convert_fusion.13
  384.8 30.6 %attend_backward.3 = (bf16[3,256,768]{2,1,0:T(8,128)(2,1)}, f32[1,768]{1,0:T(1,128)}, f32[1,768]{1,0:T(1,128)}, f32[1,2304]{1,0:T(1,128)}, bf16[1,192,3072]{2,1,...) custom-call(s32[6]{0:T(128)} %pad_add_fusion.info, ...), custom_call_target="tpu_custom_call" | custom-call | flops 30000001024 | bytes 30000000 | tf_op jit(solution)/shard_map/attend_backward/pallas_call | solution.py:432
  417.2 4.5 collective-permute-done.60
  428.6 2.1 collective-permute-start.65
  431.2 2.1 add_convert_fusion.11
  437.5 2.3 fusion.13
  442.0 9.7 %collective-permute-done.77 = bf16[2,48,3072]{2,1,0:T(8,128)(2,1)S(1)} collective-permute-done((bf16[2,48,3072]{2,1,0:T(8,128)(2,1)S(1)}, bf16[2,48,3072]{2,1,0:T(8,128)(2,1)S(1)}, u32[]{:S(2)}, u32[]{:S(2)}) %collective-permute-start.77) | collective-permute-done | bytes 589856 | tf_op jit(solution)/shard_map/ppermute | solution.py:914
  451.7 2.2 add_convert_fusion.8
  454.0 18.2 %all-reduce.5.cloned.1.call-done = bf16[4,96,3072]{2,1,0:T(8,128)(2,1)} async-done(((bf16[4,96,3072]{2,1,0:T(8,128)(2,1)}), bf16[4,96,3072]{2,1,0:T(8,128)(2,1)}) %all-reduce.5.cloned.1.call-update) | async-done | bytes 2359312 | tf_op jit(solution)/shard_map/psum | solution.py:1351
  479.4 7.3 %collective-permute-done.79 = bf16[2,96,1536]{2,1,0:T(8,128)(2,1)S(1)} collective-permute-done((bf16[2,96,1536]{2,1,0:T(8,128)(2,1)S(1)}, bf16[2,96,1536]{2,1,0:T(8,128)(2,1)S(1)}, u32[]{:S(2)}, u32[]{:S(2)}) %collective-permute-start.79) | collective-permute-done | bytes 589856 | tf_op jit(solution)/shard_map/ppermute | solution.py:922
  487.7 5.0 collective-permute-done.69
  492.7 2.3 fusion.7
  495.9 6.7 %collective-permute-done.80 = bf16[2,96,768]{2,1,0:T(8,128)(2,1)S(1)} collective-permute-done((bf16[2,96,768]{2,1,0:T(8,128)(2,1)S(1)}, bf16[2,96,768]{2,1,0:T(8,128)(2,1)S(1)}, u32[]{:S(2)}, u32[]{:S(2)}) %collective-permute-start.80) | collective-permute-done | bytes 294944 | tf_op jit(solution)/shard_map/ppermute | solution.py:922
  504.8 2.7 collective-permute-start.84
  507.5 6.0 collective-permute-done.81
  513.5 2.5 collective-permute-start.82
  516.0 6.6 %collective-permute-done.71 = bf16[200,1536]{1,0:T(8,128)(2,1)S(1)} collective-permute-done((bf16[200,1536]{1,0:T(8,128)(2,1)S(1)}, bf16[200,1536]{1,0:T(8,128)(2,1)S(1)}, u32[]{:S(2)}, u32[]{:S(2)}) %collective-permute-start.71) | collective-permute-done | bytes 614432 | tf_op jit(solution)/shard_map/ppermute | solution.py:922
  524.1 2.0 pad_maximum_fusion.13
  528.4 3.8 collective-permute-done.72
  532.2 2.6 collective-permute-start.73
  534.8 11.3 %collective-permute-done.82 = bf16[2,96,1536]{2,1,0:T(8,128)(2,1)S(1)} collective-permute-done((bf16[2,96,1536]{2,1,0:T(8,128)(2,1)S(1)}, bf16[2,96,1536]{2,1,0:T(8,128)(2,1)S(1)}, u32[]{:S(2)}, u32[]{:S(2)}) %collective-permute-start.82) | collective-permute-done | bytes 589856 | tf_op jit(solution)/shard_map/ppermute | solution.py:922
  550.9 2.6 collective-permute-done.73
  553.9 14.1 %collective-permute-done.74 = bf16[200,1536]{1,0:T(8,128)(2,1)S(1)} collective-permute-done((bf16[200,1536]{1,0:T(8,128)(2,1)S(1)}, bf16[200,1536]{1,0:T(8,128)(2,1)S(1)}, u32[]{:S(2)}, u32[]{:S(2)}) %collective-permute-start.74) | collective-permute-done | bytes 614432 | tf_op jit(solution)/shard_map/ppermute | solution.py:922
  571.1 4.1 collective-permute-done.85
  575.3 2.3 collective-permute-start.90
  579.1 22.6 %collective-permute-done.86 = bf16[2,96,3072]{2,1,0:T(8,128)(2,1)S(1)} collective-permute-done((bf16[2,96,3072]{2,1,0:T(8,128)(2,1)S(1)}, bf16[2,96,3072]{2,1,0:T(8,128)(2,1)S(1)}, u32[]{:S(2)}, u32[]{:S(2)}) %collective-permute-start.86) | collective-permute-done | bytes 1179680 | tf_op jit(solution)/shard_map/ppermute | solution.py:914
  605.5 2.2 collective-permute-start.93
  612.4 12.3 %finish.2 = (f32[1,768,3072]{2,1,0:T(8,128)}, f32[1,3072,768]{2,1,0:T(8,128)}) custom-call(s32[6]{0:T(128)} %pad_add_fusion.info, f32[1,1]{1,0:T(1,128)} %bitcast.29.scale_ref, bf16[2,96,3072]{2,1,0:T(8,128)(2,1)} %copy-done.15, bf16[2,96,3072]{2,1,0:T(8,128)(2,1)} %copy-done.16, bf16[2,96,3072]{2,1,0:T(8,128)(2,1)} %copy-done.17, ...), custom_call_target="tpu_custom_call" | custom-call | bytes 100000 | tf_op jit(solution)/shard_map/finish/pallas_call | solution.py:858
  630.6 8.6 %finish.3 = (f32[1,768,2304]{2,1,0:T(8,128)}, f32[1,768,768]{2,1,0:T(8,128)}) custom-call(s32[6]{0:T(128)} %pad_add_fusion.info, f32[1,1]{1,0:T(1,128)} %bitcast.25.scale_ref, bf16[1,96,3072]{2,1,0:T(8,128)(2,1)} %copy-done.23, bf16[1,96,3072]{2,1,0:T(8,128)(2,1)} %copy-done.19, bf16[1,96,3072]{2,1,0:T(8,128)(2,1)} %copy-done.20, ...), custom_call_target="tpu_custom_call" | custom-call | bytes 100000 | tf_op jit(solution)/shard_map/finish/pallas_call | solution.py:858
  (425 shorter events, 126.8 us)
Async XLA Ops:
  7.2 465.0 %all-reduce.5.cloned.1.call-start = ((), (), s32[]{:S(2)}) async-start(), calls=%async_computation | async-start | bytes 4718592 | tf_op jit(solution)/shard_map/psum | solution.py:1351
  12.5 29.4 %collective-permute-start.3 = (bf16[2,384,768]{2,1,0:T(8,128)(2,1)}, bf16[2,384,768]{2,1,0:T(8,128)(2,1)S(1)}, u32[]{:S(2)}, u32[]{:S(2)}) collective-permute-start(bf16[2,384,768]{2,1,0:T(8,128)(2,1)} %get-tuple-element.286), channel_id=1, source_target_pairs={{0,8},{8,0},{16,24},{24,16},{1,9},{9,1},{17,25},{25,17},{2,10},{10... | collective-permute-start | bytes 3538952 | tf_op jit(solution)/shard_map/ppermute | solution.py:914
  12.8 29.1 %collective-permute-start.4 = (bf16[2,384,768]{2,1,0:T(8,128)(2,1)}, bf16[2,384,768]{2,1,0:T(8,128)(2,1)S(1)}, u32[]{:S(2)}, u32[]{:S(2)}) collective-permute-start(bf16[2,384,768]{2,1,0:T(8,128)(2,1)} %get-tuple-element.287), channel_id=1, source_target_pairs={{0,16},{8,24},{16,0},{24,8},{1,17},{9,25},{17,1},{25,9},{2,18},{10... | collective-permute-start | bytes 3538952 | tf_op jit(solution)/shard_map/ppermute | solution.py:914
  15.5 24.9 %collective-permute-start = (f32[1,9344]{1,0:T(1,128)S(1)}, f32[1,9344]{1,0:T(1,128)}, u32[]{:S(2)}, u32[]{:S(2)}) collective-permute-start(f32[1,9344]{1,0:T(1,128)S(1)} %constant_dynamic-update-slice_fusion), channel_id=1, source_target_pairs={{0,8},{8,0},{16,24},{24,16},{1,9},{9,1},{17,25},{25,17},{2,10},{10... | collective-permute-start | bytes 112136 | tf_op jit(solution)/shard_map/ppermute | solution.py:914
  16.8 23.6 %collective-permute-start.1 = (f32[1,9344]{1,0:T(1,128)S(1)}, f32[1,9344]{1,0:T(1,128)}, u32[]{:S(2)}, u32[]{:S(2)}) collective-permute-start(f32[1,9344]{1,0:T(1,128)S(1)} %constant_dynamic-update-slice_fusion), channel_id=1, source_target_pairs={{0,16},{8,24},{16,0},{24,8},{1,17},{9,25},{17,1},{25,9},{2,18},{10... | collective-permute-start | bytes 112136 | tf_op jit(solution)/shard_map/ppermute | solution.py:914
  17.0 24.9 %collective-permute-start.2 = (f32[1,9344]{1,0:T(1,128)S(1)}, f32[1,9344]{1,0:T(1,128)}, u32[]{:S(2)}, u32[]{:S(2)}) collective-permute-start(f32[1,9344]{1,0:T(1,128)S(1)} %constant_dynamic-update-slice_fusion), channel_id=1, source_target_pairs={{0,24},{8,16},{16,8},{24,0},{1,25},{9,17},{17,9},{25,1},{2,26},{10... | collective-permute-start | bytes 112136 | tf_op jit(solution)/shard_map/ppermute | solution.py:914
  41.9 43.7 %collective-permute-start.8 = (bf16[2,384,768]{2,1,0:T(8,128)(2,1)S(1)}, bf16[2,384,768]{2,1,0:T(8,128)(2,1)S(1)}, u32[]{:S(2)}, u32[]{:S(2)}) collective-permute-start(bf16[2,384,768]{2,1,0:T(8,128)(2,1)S(1)} %collective-permute-done.3.refs_5_.refs_4_.refs_12_), channel_id=1, source_target_pairs={{0,1},{1,0},{2,3},{3,2},{4,5},{5,4},{6,7},{7,6},{8,9},{9,8},{10,11... | collective-permute-start | bytes 3538952 | tf_op jit(solution)/shard_map/ppermute | solution.py:918
  47.6 39.7 %collective-permute-start.9 = (bf16[2,384,768]{2,1,0:T(8,128)(2,1)}, bf16[2,384,768]{2,1,0:T(8,128)(2,1)}, u32[]{:S(2)}, u32[]{:S(2)}) collective-permute-start(bf16[2,384,768]{2,1,0:T(8,128)(2,1)} %copy-done.1), channel_id=1, source_target_pairs={{0,1},{1,0},{2,3},{3,2},{4,5},{5,4},{6,7},{7,6},{8,9},{9,8},{10,11... | collective-permute-start | bytes 3538952 | tf_op jit(solution)/shard_map/ppermute | solution.py:918
  49.0 27.9 %collective-permute-start.5 = (bf16[2,384,768]{2,1,0:T(8,128)(2,1)}, bf16[2,384,768]{2,1,0:T(8,128)(2,1)}, u32[]{:S(2)}, u32[]{:S(2)}) collective-permute-start(bf16[2,384,768]{2,1,0:T(8,128)(2,1)} %get-tuple-element.294), channel_id=1, source_target_pairs={{0,8},{8,0},{16,24},{24,16},{1,9},{9,1},{17,25},{25,17},{2,10},{10... | collective-permute-start | bytes 3538952 | tf_op jit(solution)/shard_map/ppermute | solution.py:914
  49.6 27.5 %collective-permute-start.6 = (bf16[2,384,768]{2,1,0:T(8,128)(2,1)}, bf16[2,384,768]{2,1,0:T(8,128)(2,1)}, u32[]{:S(2)}, u32[]{:S(2)}) collective-permute-start(bf16[2,384,768]{2,1,0:T(8,128)(2,1)} %get-tuple-element.295), channel_id=1, source_target_pairs={{0,16},{8,24},{16,0},{24,8},{1,17},{9,25},{17,1},{25,9},{2,18},{10... | collective-permute-start | bytes 3538952 | tf_op jit(solution)/shard_map/ppermute | solution.py:914
  82.8 29.2 %collective-permute-start.12 = (bf16[2,384,768]{2,1,0:T(8,128)(2,1)}, bf16[2,384,768]{2,1,0:T(8,128)(2,1)S(1)}, u32[]{:S(2)}, u32[]{:S(2)}) collective-permute-start(bf16[2,384,768]{2,1,0:T(8,128)(2,1)} %get-tuple-element.319), channel_id=1, source_target_pairs={{0,8},{8,0},{16,24},{1,9},{9,1},{17,25},{2,10},{10,2},{18,26},{3,1... | collective-permute-start | bytes 3538952 | tf_op jit(solution)/shard_map/ppermute | solution.py:914
  85.7 26.7 %collective-permute-start.13 = (bf16[2,384,768]{2,1,0:T(8,128)(2,1)}, bf16[2,384,768]{2,1,0:T(8,128)(2,1)S(1)}, u32[]{:S(2)}, u32[]{:S(2)}) collective-permute-start(bf16[2,384,768]{2,1,0:T(8,128)(2,1)} %get-tuple-element.320), channel_id=1, source_target_pairs={{0,16},{8,24},{16,0},{1,17},{9,25},{17,1},{2,18},{10,26},{18,2},{3... | collective-permute-start | bytes 3538952 | tf_op jit(solution)/shard_map/ppermute | solution.py:914
  89.0 29.5 %collective-permute-start.17 = (bf16[2,384,768]{2,1,0:T(8,128)(2,1)}, bf16[2,384,768]{2,1,0:T(8,128)(2,1)}, u32[]{:S(2)}, u32[]{:S(2)}) collective-permute-start(bf16[2,384,768]{2,1,0:T(8,128)(2,1)} %get-tuple-element.368.refs_4_), channel_id=1, source_target_pairs={{0,2},{2,4},{4,6},{1,3},{3,5},{5,7},{8,10},{10,12},{12,14},{9,11},... | collective-permute-start | bytes 3538952 | tf_op jit(solution)/shard_map/ppermute | solution.py:922
  90.9 34.3 %collective-permute-start.18 = (bf16[2,384,768]{2,1,0:T(8,128)(2,1)}, bf16[2,384,768]{2,1,0:T(8,128)(2,1)}, u32[]{:S(2)}, u32[]{:S(2)}) collective-permute-start(bf16[2,384,768]{2,1,0:T(8,128)(2,1)} %get-tuple-element.368.refs_4_), channel_id=1, source_target_pairs={{6,4},{4,2},{2,0},{7,5},{5,3},{3,1},{14,12},{12,10},{10,8},{15,13}... | collective-permute-start | bytes 3538952 | tf_op jit(solution)/shard_map/ppermute | solution.py:922
  112.4 20.6 %collective-permute-start.23 = (bf16[2,384,768]{2,1,0:T(8,128)(2,1)S(1)}, bf16[2,384,768]{2,1,0:T(8,128)(2,1)S(1)}, u32[]{:S(2)}, u32[]{:S(2)}) collective-permute-start(bf16[2,384,768]{2,1,0:T(8,128)(2,1)S(1)} %collective-permute-done.12.refs_6_.refs_8_.refs_14_), channel_id=1, source_target_pairs={{0,1},{1,0},{2,3},{3,2},{4,5},{5,4},{6,7},{7,6},{8,9},{9,8},{10,11... | collective-permute-start | bytes 3538952 | tf_op jit(solution)/shard_map/ppermute | solution.py:918
  125.2 21.6 %collective-permute-start.24 = (bf16[2,384,768]{2,1,0:T(8,128)(2,1)}, bf16[2,384,768]{2,1,0:T(8,128)(2,1)S(1)}, u32[]{:S(2)}, u32[]{:S(2)}) collective-permute-start(bf16[2,384,768]{2,1,0:T(8,128)(2,1)} %copy-done.3), channel_id=1, source_target_pairs={{0,1},{1,0},{2,3},{3,2},{4,5},{5,4},{6,7},{7,6},{8,9},{9,8},{10,11... | collective-permute-start | bytes 3538952 | tf_op jit(solution)/shard_map/ppermute | solution.py:918
  128.6 26.8 %collective-permute-start.19 = (bf16[2,384,768]{2,1,0:T(8,128)(2,1)}, bf16[2,384,768]{2,1,0:T(8,128)(2,1)S(1)}, u32[]{:S(2)}, u32[]{:S(2)}) collective-permute-start(bf16[2,384,768]{2,1,0:T(8,128)(2,1)} %get-tuple-element.341), channel_id=1, source_target_pairs={{0,8},{8,0},{16,24},{24,16},{1,9},{9,1},{17,25},{25,17},{2,10},{10... | collective-permute-start | bytes 3538952 | tf_op jit(solution)/shard_map/ppermute | solution.py:914
  129.3 28.0 %collective-permute-start.20 = (bf16[2,384,768]{2,1,0:T(8,128)(2,1)}, bf16[2,384,768]{2,1,0:T(8,128)(2,1)S(1)}, u32[]{:S(2)}, u32[]{:S(2)}) collective-permute-start(bf16[2,384,768]{2,1,0:T(8,128)(2,1)} %get-tuple-element.342), channel_id=1, source_target_pairs={{0,16},{8,24},{24,8},{1,17},{9,25},{25,9},{2,18},{10,26},{26,10},{... | collective-permute-start | bytes 3538952 | tf_op jit(solution)/shard_map/ppermute | solution.py:914
  131.7 28.0 %collective-permute-start.21 = (bf16[2,384,768]{2,1,0:T(8,128)(2,1)}, bf16[2,384,768]{2,1,0:T(8,128)(2,1)}, u32[]{:S(2)}, u32[]{:S(2)}) collective-permute-start(bf16[2,384,768]{2,1,0:T(8,128)(2,1)} %collective-permute-done.17.refs_12_), channel_id=1, source_target_pairs={{2,4},{4,6},{3,5},{5,7},{10,12},{12,14},{11,13},{13,15},{18,20},{2... | collective-permute-start | bytes 3538952 | tf_op jit(solution)/shard_map/ppermute | solution.py:922
  133.0 26.7 %collective-permute-start.22 = (bf16[2,384,768]{2,1,0:T(8,128)(2,1)}, bf16[2,384,768]{2,1,0:T(8,128)(2,1)S(1)}, u32[]{:S(2)}, u32[]{:S(2)}) collective-permute-start(bf16[2,384,768]{2,1,0:T(8,128)(2,1)} %collective-permute-done.18.refs_6_), channel_id=1, source_target_pairs={{4,2},{2,0},{5,3},{3,1},{12,10},{10,8},{13,11},{11,9},{20,18},{18,... | collective-permute-start | bytes 3538952 | tf_op jit(solution)/shard_map/ppermute | solution.py:922
  163.3 30.1 %collective-permute-start.30 = (bf16[2,384,768]{2,1,0:T(8,128)(2,1)}, bf16[2,384,768]{2,1,0:T(8,128)(2,1)}, u32[]{:S(2)}, u32[]{:S(2)}) collective-permute-start(bf16[2,384,768]{2,1,0:T(8,128)(2,1)} %collective-permute-done.21.refs_14_), channel_id=1, source_target_pairs={{4,6},{5,7},{12,14},{13,15},{20,22},{21,23},{28,30},{29,31}} | collective-permute-start | bytes 3538952 | tf_op jit(solution)/shard_map/ppermute | solution.py:922
  164.6 28.8 %collective-permute-start.31 = (bf16[2,384,768]{2,1,0:T(8,128)(2,1)}, bf16[2,384,768]{2,1,0:T(8,128)(2,1)}, u32[]{:S(2)}, u32[]{:S(2)}) collective-permute-start(bf16[2,384,768]{2,1,0:T(8,128)(2,1)} %copy-done.11), channel_id=1, source_target_pairs={{2,0},{3,1},{10,8},{11,9},{18,16},{19,17},{26,24},{27,25}} | collective-permute-start | bytes 3538952 | tf_op jit(solution)/shard_map/ppermute | solution.py:922
  166.3 24.0 %collective-permute-start.27 = (bf16[144,768]{1,0:T(8,128)(2,1)}, bf16[144,768]{1,0:T(8,128)(2,1)S(1)}, u32[]{:S(2)}, u32[]{:S(2)}) collective-permute-start(bf16[144,768]{1,0:T(8,128)(2,1)} %get-tuple-element.360), channel_id=1, source_target_pairs={{0,8},{1,9},{2,10},{3,11},{4,12},{5,13},{6,14},{7,15}} | collective-permute-start | bytes 663560 | tf_op jit(solution)/shard_map/ppermute | solution.py:914
  167.6 22.7 %collective-permute-start.28 = (bf16[144,768]{1,0:T(8,128)(2,1)}, bf16[144,768]{1,0:T(8,128)(2,1)}, u32[]{:S(2)}, u32[]{:S(2)}) collective-permute-start(bf16[144,768]{1,0:T(8,128)(2,1)} %get-tuple-element.361), channel_id=1, source_target_pairs={{0,16},{1,17},{2,18},{3,19},{4,20},{5,21},{6,22},{7,23}} | collective-permute-start | bytes 663560 | tf_op jit(solution)/shard_map/ppermute | solution.py:914
  169.0 21.3 %collective-permute-start.29 = (bf16[144,768]{1,0:T(8,128)(2,1)}, bf16[144,768]{1,0:T(8,128)(2,1)}, u32[]{:S(2)}, u32[]{:S(2)}) collective-permute-start(bf16[144,768]{1,0:T(8,128)(2,1)} %get-tuple-element.362), channel_id=1, source_target_pairs={{0,24},{1,25},{2,26},{3,27},{4,28},{5,29},{6,30},{7,31}} | collective-permute-start | bytes 663560 | tf_op jit(solution)/shard_map/ppermute | solution.py:914
  195.1 22.1 %collective-permute-start.35 = (bf16[2,384,768]{2,1,0:T(8,128)(2,1)}, bf16[2,384,768]{2,1,0:T(8,128)(2,1)S(1)}, u32[]{:S(2)}, u32[]{:S(2)}) collective-permute-start(bf16[2,384,768]{2,1,0:T(8,128)(2,1)} %collective-permute-done.18.refs_6_), channel_id=1, source_target_pairs={{0,1},{1,0},{2,3},{3,2},{4,5},{5,4},{6,7},{7,6},{8,9},{9,8},{10,11... | collective-permute-start | bytes 3538952 | tf_op jit(solution)/shard_map/ppermute | solution.py:918
  195.9 21.3 %collective-permute-start.36 = (bf16[2,384,768]{2,1,0:T(8,128)(2,1)}, bf16[2,384,768]{2,1,0:T(8,128)(2,1)}, u32[]{:S(2)}, u32[]{:S(2)}) collective-permute-start(bf16[2,384,768]{2,1,0:T(8,128)(2,1)} %get-tuple-element.368.refs_4_), channel_id=1, source_target_pairs={{0,1},{1,0},{2,3},{3,2},{4,5},{5,4},{6,7},{7,6},{8,9},{9,8},{10,11... | collective-permute-start | bytes 3538952 | tf_op jit(solution)/shard_map/ppermute | solution.py:918
  197.0 20.2 %collective-permute-start.37 = (bf16[2,384,768]{2,1,0:T(8,128)(2,1)}, bf16[2,384,768]{2,1,0:T(8,128)(2,1)}, u32[]{:S(2)}, u32[]{:S(2)}) collective-permute-start(bf16[2,384,768]{2,1,0:T(8,128)(2,1)} %collective-permute-done.17.refs_12_), channel_id=1, source_target_pairs={{0,1},{1,0},{2,3},{3,2},{4,5},{5,4},{6,7},{7,6},{8,9},{9,8},{10,11... | collective-permute-start | bytes 3538952 | tf_op jit(solution)/shard_map/ppermute | solution.py:918
  198.6 18.6 %collective-permute-start.38 = (bf16[2,384,768]{2,1,0:T(8,128)(2,1)}, bf16[2,384,768]{2,1,0:T(8,128)(2,1)}, u32[]{:S(2)}, u32[]{:S(2)}) collective-permute-start(bf16[2,384,768]{2,1,0:T(8,128)(2,1)} %collective-permute-done.21.refs_14_), channel_id=1, source_target_pairs={{0,1},{1,0},{2,3},{3,2},{4,5},{5,4},{6,7},{7,6},{8,9},{9,8},{10,11... | collective-permute-start | bytes 3538952 | tf_op jit(solution)/shard_map/ppermute | solution.py:918
  217.2 24.1 %collective-permute-start.40 = (f32[1,128]{1,0:T(1,128)S(1)}, f32[1,128]{1,0:T(1,128)S(1)}, u32[]{:S(2)}, u32[]{:S(2)}) collective-permute-start(f32[1,128]{1,0:T(1,128)S(1)} %add.246), channel_id=1, source_target_pairs={{0,4},{2,6},{4,0},{6,2},{1,5},{3,7},{5,1},{7,3},{8,12},{10,14},{12... | collective-permute-start | bytes 1544 | tf_op jit(solution)/shard_map/ppermute | solution.py:922
  241.9 33.9 %collective-permute-start.41 = (bf16[2,384,768]{2,1,0:T(8,128)(2,1)S(1)}, bf16[2,384,768]{2,1,0:T(8,128)(2,1)}, u32[]{:S(2)}, u32[]{:S(2)}) collective-permute-start(bf16[2,384,768]{2,1,0:T(8,128)(2,1)S(1)} %copy-done.75), channel_id=1, source_target_pairs={{0,16},{8,24},{1,17},{9,25},{2,18},{10,26},{3,19},{11,27},{4,20},{... | collective-permute-start | bytes 3538952 | tf_op jit(solution)/shard_map/ppermute | solution.py:914
  276.5 40.4 %collective-permute-start.45 = (bf16[2,192,3072]{2,1,0:T(8,128)(2,1)}, bf16[2,192,3072]{2,1,0:T(8,128)(2,1)S(1)}, u32[]{:S(2)}, u32[]{:S(2)}) collective-permute-start(bf16[2,192,3072]{2,1,0:T(8,128)(2,1)} %get-tuple-element.441), channel_id=1, source_target_pairs={{0,1},{1,0},{2,3},{3,2},{4,5},{5,4},{6,7},{7,6},{8,9},{9,8},{10,11... | collective-permute-start | bytes 7077896 | tf_op jit(solution)/shard_map/ppermute | solution.py:918
  276.6 40.3 %collective-permute-start.46 = (bf16[2,384,768]{2,1,0:T(8,128)(2,1)}, bf16[2,384,768]{2,1,0:T(8,128)(2,1)}, u32[]{:S(2)}, u32[]{:S(2)}) collective-permute-start(bf16[2,384,768]{2,1,0:T(8,128)(2,1)} %collective-permute-done.41.refs_6_), channel_id=1, source_target_pairs={{0,1},{1,0},{2,3},{3,2},{4,5},{5,4},{6,7},{7,6},{8,9},{9,8},{10,11... | collective-permute-start | bytes 3538952 | tf_op jit(solution)/shard_map/ppermute | solution.py:918
  284.8 32.1 %collective-permute-start.43 = (bf16[2,96,3072]{2,1,0:T(8,128)(2,1)}, bf16[2,96,3072]{2,1,0:T(8,128)(2,1)S(1)}, u32[]{:S(2)}, u32[]{:S(2)}) collective-permute-start(bf16[2,96,3072]{2,1,0:T(8,128)(2,1)} %get-tuple-element.574), channel_id=1, source_target_pairs={{0,8},{8,0},{16,24},{24,16},{1,9},{9,1},{17,25},{25,17},{2,10},{10... | collective-permute-start | bytes 3538952 | tf_op jit(solution)/shard_map/ppermute | solution.py:914
  287.5 29.4 %collective-permute-start.44 = (bf16[2,96,3072]{2,1,0:T(8,128)(2,1)}, bf16[2,96,3072]{2,1,0:T(8,128)(2,1)}, u32[]{:S(2)}, u32[]{:S(2)}) collective-permute-start(bf16[2,96,3072]{2,1,0:T(8,128)(2,1)} %get-tuple-element.573), channel_id=1, source_target_pairs={{0,16},{8,24},{16,0},{24,8},{1,17},{9,25},{17,1},{25,9},{2,18},{10... | collective-permute-start | bytes 3538952 | tf_op jit(solution)/shard_map/ppermute | solution.py:914
  316.9 35.3 %collective-permute-start.47 = (bf16[144,768]{1,0:T(8,128)(2,1)}, bf16[144,768]{1,0:T(8,128)(2,1)S(1)}, u32[]{:S(2)}, u32[]{:S(2)}) collective-permute-start(bf16[144,768]{1,0:T(8,128)(2,1)} %bitcast.118), channel_id=1, source_target_pairs={{0,8},{8,0},{16,24},{24,16},{1,9},{9,1},{17,25},{25,17},{2,10},{10... | collective-permute-start | bytes 663560 | tf_op jit(solution)/shard_map/ppermute | solution.py:914
  317.0 35.2 %collective-permute-start.48 = (bf16[144,768]{1,0:T(8,128)(2,1)}, bf16[144,768]{1,0:T(8,128)(2,1)}, u32[]{:S(2)}, u32[]{:S(2)}) collective-permute-start(bf16[144,768]{1,0:T(8,128)(2,1)} %bitcast.119), channel_id=1, source_target_pairs={{0,16},{8,24},{16,0},{24,8},{1,17},{9,25},{17,1},{25,9},{2,18},{10... | collective-permute-start | bytes 663560 | tf_op jit(solution)/shard_map/ppermute | solution.py:914
  318.4 33.9 %collective-permute-start.49 = (bf16[144,768]{1,0:T(8,128)(2,1)}, bf16[144,768]{1,0:T(8,128)(2,1)}, u32[]{:S(2)}, u32[]{:S(2)}) collective-permute-start(bf16[144,768]{1,0:T(8,128)(2,1)} %bitcast.120), channel_id=1, source_target_pairs={{0,24},{8,16},{16,8},{24,0},{1,25},{9,17},{17,9},{25,1},{2,26},{10... | collective-permute-start | bytes 663560 | tf_op jit(solution)/shard_map/ppermute | solution.py:914
  322.3 45.3 %collective-permute-start.50 = (bf16[2,48,3072]{2,1,0:T(8,128)(2,1)}, bf16[2,48,3072]{2,1,0:T(8,128)(2,1)}, u32[]{:S(2)}, u32[]{:S(2)}) collective-permute-start(bf16[2,48,3072]{2,1,0:T(8,128)(2,1)} %get-tuple-element.571), channel_id=1, source_target_pairs={{0,16},{8,24},{16,0},{24,8},{1,17},{9,25},{17,1},{25,9},{2,18},{10... | collective-permute-start | bytes 1769480 | tf_op jit(solution)/shard_map/ppermute | solution.py:914
  323.6 45.6 %collective-permute-start.51 = (bf16[2,48,3072]{2,1,0:T(8,128)(2,1)}, bf16[2,48,3072]{2,1,0:T(8,128)(2,1)}, u32[]{:S(2)}, u32[]{:S(2)}) collective-permute-start(bf16[2,48,3072]{2,1,0:T(8,128)(2,1)} %get-tuple-element.572), channel_id=1, source_target_pairs={{0,8},{8,0},{16,24},{24,16},{1,9},{9,1},{17,25},{25,17},{2,10},{10... | collective-permute-start | bytes 1769480 | tf_op jit(solution)/shard_map/ppermute | solution.py:914
  376.8 54.4 %collective-permute-start.63 = (bf16[2,192,3072]{2,1,0:T(8,128)(2,1)}, bf16[2,192,3072]{2,1,0:T(8,128)(2,1)}, u32[]{:S(2)}, u32[]{:S(2)}) collective-permute-start(bf16[2,192,3072]{2,1,0:T(8,128)(2,1)} %get-tuple-element.506), channel_id=1, source_target_pairs={{0,1},{1,0},{2,3},{3,2},{4,5},{5,4},{6,7},{7,6},{8,9},{9,8},{10,11... | collective-permute-start | bytes 7077896 | tf_op jit(solution)/shard_map/ppermute | solution.py:918
  381.8 33.6 %collective-permute-start.58 = (bf16[1,96,3072]{2,1,0:T(8,128)(2,1)}, bf16[1,96,3072]{2,1,0:T(8,128)(2,1)}, u32[]{:S(2)}, u32[]{:S(2)}) collective-permute-start(bf16[1,96,3072]{2,1,0:T(8,128)(2,1)} %get-tuple-element.489), channel_id=1, source_target_pairs={{0,8},{8,0},{16,24},{24,16},{1,9},{9,1},{17,25},{25,17},{2,10},{10... | collective-permute-start | bytes 1769480 | tf_op jit(solution)/shard_map/ppermute | solution.py:914
  383.2 34.0 %collective-permute-start.59 = (bf16[1,96,3072]{2,1,0:T(8,128)(2,1)}, bf16[1,96,3072]{2,1,0:T(8,128)(2,1)}, u32[]{:S(2)}, u32[]{:S(2)}) collective-permute-start(bf16[1,96,3072]{2,1,0:T(8,128)(2,1)} %get-tuple-element.490), channel_id=1, source_target_pairs={{0,16},{8,24},{16,0},{24,8},{1,17},{9,25},{17,1},{25,9},{2,18},{10... | collective-permute-start | bytes 1769480 | tf_op jit(solution)/shard_map/ppermute | solution.py:914
  383.3 38.4 %collective-permute-start.60 = (bf16[2,96,3072]{2,1,0:T(8,128)(2,1)S(1)}, bf16[2,96,3072]{2,1,0:T(8,128)(2,1)S(1)}, u32[]{:S(2)}, u32[]{:S(2)}) collective-permute-start(bf16[2,96,3072]{2,1,0:T(8,128)(2,1)S(1)} %get-tuple-element.484), channel_id=1, source_target_pairs={{0,8},{8,0},{16,24},{24,16},{1,9},{9,1},{17,25},{25,17},{2,10},{10... | collective-permute-start | bytes 3538952 | tf_op jit(solution)/shard_map/ppermute | solution.py:914
  383.5 38.9 %collective-permute-start.61 = (bf16[2,96,3072]{2,1,0:T(8,128)(2,1)S(1)}, bf16[2,96,3072]{2,1,0:T(8,128)(2,1)}, u32[]{:S(2)}, u32[]{:S(2)}) collective-permute-start(bf16[2,96,3072]{2,1,0:T(8,128)(2,1)S(1)} %get-tuple-element.485), channel_id=1, source_target_pairs={{0,16},{8,24},{16,0},{24,8},{1,17},{9,25},{17,1},{25,9},{2,18},{10... | collective-permute-start | bytes 3538952 | tf_op jit(solution)/shard_map/ppermute | solution.py:914
  415.4 21.8 %collective-permute-start.68 = (bf16[1,192,3072]{2,1,0:T(8,128)(2,1)}, bf16[1,192,3072]{2,1,0:T(8,128)(2,1)}, u32[]{:S(2)}, u32[]{:S(2)}) collective-permute-start(bf16[1,192,3072]{2,1,0:T(8,128)(2,1)} %get-tuple-element.533), channel_id=1, source_target_pairs={{0,1},{1,0},{2,3},{3,2},{4,5},{5,4},{6,7},{7,6},{8,9},{9,8},{10,11... | collective-permute-start | bytes 3538952 | tf_op jit(solution)/shard_map/ppermute | solution.py:918
  430.7 43.8 %collective-permute-start.62 = (bf16[1,192,3072]{2,1,0:T(8,128)(2,1)}, bf16[1,192,3072]{2,1,0:T(8,128)(2,1)}, u32[]{:S(2)}, u32[]{:S(2)}) collective-permute-start(bf16[1,192,3072]{2,1,0:T(8,128)(2,1)} %get-tuple-element.504), channel_id=1, source_target_pairs={{0,1},{1,0},{2,3},{3,2},{4,5},{5,4},{6,7},{7,6},{8,9},{9,8},{10,11... | collective-permute-start | bytes 3538952 | tf_op jit(solution)/shard_map/ppermute | solution.py:918
  439.7 33.6 %collective-permute-start.66 = (bf16[104,3072]{1,0:T(8,128)(2,1)}, bf16[104,3072]{1,0:T(8,128)(2,1)}, u32[]{:S(2)}, u32[]{:S(2)}) collective-permute-start(bf16[104,3072]{1,0:T(8,128)(2,1)} %pad_maximum_fusion.4), channel_id=1, source_target_pairs={{0,8},{8,0},{16,24},{24,16},{1,9},{9,1},{17,25},{25,17},{2,10},{10... | collective-permute-start | bytes 1916936 | tf_op jit(solution)/shard_map/ppermute | solution.py:914
  440.7 33.8 %collective-permute-start.67 = (bf16[1,96,3072]{2,1,0:T(8,128)(2,1)}, bf16[1,96,3072]{2,1,0:T(8,128)(2,1)}, u32[]{:S(2)}, u32[]{:S(2)}) collective-permute-start(bf16[1,96,3072]{2,1,0:T(8,128)(2,1)} %get-tuple-element.530), channel_id=1, source_target_pairs={{0,16},{8,24},{16,0},{24,8},{1,17},{9,25},{17,1},{25,9},{2,18},{10... | collective-permute-start | bytes 1769480 | tf_op jit(solution)/shard_map/ppermute | solution.py:914
  495.2 27.4 %collective-permute-start.71 = (bf16[200,1536]{1,0:T(8,128)(2,1)S(1)}, bf16[200,1536]{1,0:T(8,128)(2,1)S(1)}, u32[]{:S(2)}, u32[]{:S(2)}) collective-permute-start(bf16[200,1536]{1,0:T(8,128)(2,1)S(1)} %constant_dynamic-slice_fusion.8), channel_id=1, source_target_pairs={{0,2},{2,0},{4,6},{6,4},{1,3},{3,1},{5,7},{7,5},{8,10},{10,8},{12,... | collective-permute-start | bytes 1843208 | tf_op jit(solution)/shard_map/ppermute | solution.py:922
  503.0 43.2 %collective-permute-start.83 = (bf16[2,96,3072]{2,1,0:T(8,128)(2,1)S(1)}, bf16[2,96,3072]{2,1,0:T(8,128)(2,1)S(1)}, u32[]{:S(2)}, u32[]{:S(2)}) collective-permute-start(bf16[2,96,3072]{2,1,0:T(8,128)(2,1)S(1)} %get-tuple-element.577), channel_id=1, source_target_pairs={{8,0},{16,24},{9,1},{17,25},{10,2},{18,26},{11,3},{19,27},{12,4},{... | collective-permute-start | bytes 3538952 | tf_op jit(solution)/shard_map/ppermute | solution.py:914
  504.8 41.4 %collective-permute-start.84 = (bf16[2,96,3072]{2,1,0:T(8,128)(2,1)S(1)}, bf16[2,96,3072]{2,1,0:T(8,128)(2,1)S(1)}, u32[]{:S(2)}, u32[]{:S(2)}) collective-permute-start(bf16[2,96,3072]{2,1,0:T(8,128)(2,1)S(1)} %get-tuple-element.576), channel_id=1, source_target_pairs={{8,24},{16,0},{9,25},{17,1},{10,26},{18,2},{11,27},{19,3},{12,28},... | collective-permute-start | bytes 3538952 | tf_op jit(solution)/shard_map/ppermute | solution.py:914
  513.5 32.5 %collective-permute-start.82 = (bf16[2,96,1536]{2,1,0:T(8,128)(2,1)S(1)}, bf16[2,96,1536]{2,1,0:T(8,128)(2,1)S(1)}, u32[]{:S(2)}, u32[]{:S(2)}) collective-permute-start(bf16[2,96,1536]{2,1,0:T(8,128)(2,1)S(1)} %pad_maximum_fusion.11), channel_id=1, source_target_pairs={{0,2},{2,0},{4,6},{6,4},{1,3},{3,1},{5,7},{7,5},{8,10},{10,8},{12,... | collective-permute-start | bytes 1769480 | tf_op jit(solution)/shard_map/ppermute | solution.py:922
  532.2 21.3 %collective-permute-start.73 = (bf16[200,768]{1,0:T(8,128)(2,1)S(1)}, bf16[200,768]{1,0:T(8,128)(2,1)S(1)}, u32[]{:S(2)}, u32[]{:S(2)}) collective-permute-start(bf16[200,768]{1,0:T(8,128)(2,1)S(1)} %add_convert_fusion.19), channel_id=1, source_target_pairs={{0,4},{2,6},{4,0},{6,2},{1,5},{3,7},{5,1},{7,3},{8,12},{10,14},{12... | collective-permute-start | bytes 921608 | tf_op jit(solution)/shard_map/ppermute | solution.py:922
  546.2 28.9 %collective-permute-start.85 = (bf16[2,96,3072]{2,1,0:T(8,128)(2,1)S(1)}, bf16[2,96,3072]{2,1,0:T(8,128)(2,1)S(1)}, u32[]{:S(2)}, u32[]{:S(2)}) collective-permute-start(bf16[2,96,3072]{2,1,0:T(8,128)(2,1)S(1)} %pad_maximum_fusion.3), channel_id=1, source_target_pairs={{0,8},{1,9},{2,10},{3,11},{4,12},{5,13},{6,14},{7,15}} | collective-permute-start | bytes 3538952 | tf_op jit(solution)/shard_map/ppermute | solution.py:914
  547.5 54.2 %collective-permute-start.86 = (bf16[2,96,3072]{2,1,0:T(8,128)(2,1)S(1)}, bf16[2,96,3072]{2,1,0:T(8,128)(2,1)S(1)}, u32[]{:S(2)}, u32[]{:S(2)}) collective-permute-start(bf16[2,96,3072]{2,1,0:T(8,128)(2,1)S(1)} %pad_maximum_fusion.3), channel_id=1, source_target_pairs={{24,8},{25,9},{26,10},{27,11},{28,12},{29,13},{30,14},{31,15}} | collective-permute-start | bytes 3538952 | tf_op jit(solution)/shard_map/ppermute | solution.py:914
  548.8 58.9 %collective-permute-start.88 = (bf16[2,96,3072]{2,1,0:T(8,128)(2,1)S(1)}, bf16[2,96,3072]{2,1,0:T(8,128)(2,1)S(1)}, u32[]{:S(2)}, u32[]{:S(2)}) collective-permute-start(bf16[2,96,3072]{2,1,0:T(8,128)(2,1)S(1)} %pad_maximum_fusion.3), channel_id=1, source_target_pairs={{16,8},{17,9},{18,10},{19,11},{20,12},{21,13},{22,14},{23,15}} | collective-permute-start | bytes 3538952 | tf_op jit(solution)/shard_map/ppermute | solution.py:914
  550.1 55.4 %collective-permute-start.87 = (bf16[2,96,3072]{2,1,0:T(8,128)(2,1)S(1)}, bf16[2,96,3072]{2,1,0:T(8,128)(2,1)S(1)}, u32[]{:S(2)}, u32[]{:S(2)}) collective-permute-start(bf16[2,96,3072]{2,1,0:T(8,128)(2,1)S(1)} %get-tuple-element.548), channel_id=1, source_target_pairs={{0,24},{24,0},{1,25},{25,1},{2,26},{26,2},{3,27},{27,3},{4,28},{28... | collective-permute-start | bytes 3538952 | tf_op jit(solution)/shard_map/ppermute | solution.py:914
  575.3 27.3 %collective-permute-start.90 = (bf16[2,96,3072]{2,1,0:T(8,128)(2,1)S(1)}, bf16[2,96,3072]{2,1,0:T(8,128)(2,1)S(1)}, u32[]{:S(2)}, u32[]{:S(2)}) collective-permute-start(bf16[2,96,3072]{2,1,0:T(8,128)(2,1)S(1)} %select_select_fusion.2.refs_1_), channel_id=1, source_target_pairs={{0,1},{1,0},{2,3},{3,2},{4,5},{5,4},{6,7},{7,6},{8,9},{9,8},{10,11... | collective-permute-start | bytes 3538952 | tf_op jit(solution)/shard_map/ppermute | solution.py:918
  577.7 30.2 %collective-permute-start.75 = (bf16[1,96,3072]{2,1,0:T(8,128)(2,1)S(1)}, bf16[1,96,3072]{2,1,0:T(8,128)(2,1)S(1)}, u32[]{:S(2)}, u32[]{:S(2)}) collective-permute-start(bf16[1,96,3072]{2,1,0:T(8,128)(2,1)S(1)} %get-tuple-element.595), channel_id=1, source_target_pairs={{8,0},{24,16},{9,1},{25,17},{10,2},{26,18},{11,3},{27,19},{12,4},{... | collective-permute-start | bytes 1769480 | tf_op jit(solution)/shard_map/ppermute | solution.py:914
  605.5 19.1 %collective-permute-start.93 = (bf16[1,96,3072]{2,1,0:T(8,128)(2,1)}, bf16[1,96,3072]{2,1,0:T(8,128)(2,1)}, u32[]{:S(2)}, u32[]{:S(2)}) collective-permute-start(bf16[1,96,3072]{2,1,0:T(8,128)(2,1)} %get-tuple-element.558), channel_id=1, source_target_pairs={{8,16},{24,0},{9,17},{25,1},{10,18},{26,2},{11,19},{27,3},{12,20},... | collective-permute-start | bytes 1769480 | tf_op jit(solution)/shard_map/ppermute | solution.py:914
  607.7 21.5 %collective-permute-start.94 = (bf16[1,96,3072]{2,1,0:T(8,128)(2,1)S(1)}, bf16[1,96,3072]{2,1,0:T(8,128)(2,1)S(1)}, u32[]{:S(2)}, u32[]{:S(2)}) collective-permute-start(bf16[1,96,3072]{2,1,0:T(8,128)(2,1)S(1)} %get-tuple-element.596.refs_0_), channel_id=1, source_target_pairs={{0,1},{1,0},{2,3},{3,2},{4,5},{5,4},{6,7},{7,6},{8,9},{9,8},{10,11... | collective-permute-start | bytes 1769480 | tf_op jit(solution)/shard_map/ppermute | solution.py:918
  608.5 20.6 %collective-permute-start.95 = (bf16[1,96,3072]{2,1,0:T(8,128)(2,1)S(1)}, bf16[1,96,3072]{2,1,0:T(8,128)(2,1)S(1)}, u32[]{:S(2)}, u32[]{:S(2)}) collective-permute-start(bf16[1,96,3072]{2,1,0:T(8,128)(2,1)S(1)} %fusion.2.refs_1_), channel_id=1, source_target_pairs={{0,1},{1,0},{2,3},{3,2},{4,5},{5,4},{6,7},{7,6},{8,9},{9,8},{10,11... | collective-permute-start | bytes 1769480 | tf_op jit(solution)/shard_map/ppermute | solution.py:918
  609.4 19.8 %collective-permute-start.96 = (bf16[1,96,3072]{2,1,0:T(8,128)(2,1)S(1)}, bf16[1,96,3072]{2,1,0:T(8,128)(2,1)S(1)}, u32[]{:S(2)}, u32[]{:S(2)}) collective-permute-start(bf16[1,96,3072]{2,1,0:T(8,128)(2,1)S(1)} %fusion.3.refs_2_), channel_id=1, source_target_pairs={{0,1},{1,0},{2,3},{3,2},{4,5},{5,4},{6,7},{7,6},{8,9},{9,8},{10,11... | collective-permute-start | bytes 1769480 | tf_op jit(solution)/shard_map/ppermute | solution.py:918
  (114 other events, 1499.1 us)
Sparse Core Ops, SparseCore 0:
  376.9 95.2 all-reduce.4
where the time goes:
time: 655 us; the launch traced here: 646 us
  Pallas kernels  248 us (38%)
  waiting for transfers between devices  199 us (30%)
  starting transfers between devices  111 us (17%)
  other arithmetic  44.9 us (7%)
  local copies, waits for them, and re-layouts  26.8 us (4%)
  between operations  16.7 us (3%)
    ppermute x47, waiting for transfers between devices, over_section(): return lax.ppermute(value, 'section', [(at, at ^ bits) for at in sources])  106 us
    ppermute x16, waiting for transfers between devices, over_plane(): return lax.ppermute(value, 'z', pairs)  65.5 us
    pallas_call x2, Pallas kernels, attend_backward(): pl.pallas_call(partial(attend_backward_kernel, plan, len(arrays), first i...  60 us
    ppermute x47, starting transfers between devices, over_section(): return lax.ppermute(value, 'section', [(at, at ^ bits) for at in sources])  58.9 us
    pallas_call x2, Pallas kernels, expert_backward(): pl.pallas_call(partial(expert_backward_kernel, plan, len(arrays), count,...  57.6 us
    pallas_call x2, Pallas kernels, expert_forward(): pl.pallas_call(partial(expert_forward_kernel, plan, len(arrays), count, k...  41.7 us
    ppermute x35, starting transfers between devices, over_core(): return lax.ppermute(value, 'core', [(0, 1), (1, 0)])  30.7 us
    pallas_call x2, Pallas kernels, attend_forward(): pl.pallas_call(partial(attend_forward_kernel, plan, len(arrays), merge is...  27.9 us
  transfers between devices with their start and end apart: 99, of which 34 were waited for; matrix products, arithmetic and copies ran while one was open for 10% of the time, Pallas kernels for 36%

commit v1 on v0

--- a/solution.py
+++ b/solution.py
@@ -1279,7 +1279,7 @@
         language_count = lax.psum(language_count, "z")
     expert3 = weights.layer("f")
     outputs = expert_forward(
-        x3, info, expert3, row(3, 3), row(3, 4), row(3, 5), row(3, 6), ROWS, "all"
+        x3, info, expert3, row(3, 3), row(3, 4), row(3, 5), row(3, 6), 240, "all"
     )
     layer_output, act3, slope3, language_count = under([*outputs, language_count])[0]
     language_count = language_count[0, 0].astype(jnp.int32)
@@ -1309,7 +1309,7 @@
         sends, (layer_output, last_grad) = under(sends, layer_output, last_grad)
         keys = weights.move(4, sends)
     outputs = expert_backward(
-        x3, info, expert3, row(3, 3), row(3, 4), act3, slope3, last_grad, ROWS, "all"
+        x3, info, expert3, row(3, 3), row(3, 4), act3, slope3, last_grad, 240, "all"
     )
     outputs = weights.join(outputs, keys)
     crossed = weights.cross(keys)

time: 655 us -> 652 us (level)
  no operation moved by 1% of the time
where the time goes in v1:
time: 652 us; the launch traced here: 643 us
  Pallas kernels  245 us (38%)
  waiting for transfers between devices  199 us (31%)
  starting transfers between devices  111 us (17%)
  other arithmetic  44.9 us (7%)
  local copies, waits for them, and re-layouts  26.7 us (4%)
  between operations  16.7 us (3%)
    ppermute x47, waiting for transfers between devices, over_section(): return lax.ppermute(value, 'section', [(at, at ^ bits) for at in sources])  106 us
    ppermute x16, waiting for transfers between devices, over_plane(): return lax.ppermute(value, 'z', pairs)  65.5 us
    pallas_call x2, Pallas kernels, attend_backward(): pl.pallas_call(partial(attend_backward_kernel, plan, len(arrays), first i...  60 us
    ppermute x47, starting transfers between devices, over_section(): return lax.ppermute(value, 'section', [(at, at ^ bits) for at in sources])  58.7 us
    pallas_call x2, Pallas kernels, expert_backward(): pl.pallas_call(partial(expert_backward_kernel, plan, len(arrays), count,...  54.9 us
    pallas_call x2, Pallas kernels, expert_forward(): pl.pallas_call(partial(expert_forward_kernel, plan, len(arrays), count, k...  41.5 us
    ppermute x35, starting transfers between devices, over_core(): return lax.ppermute(value, 'core', [(0, 1), (1, 0)])  30.7 us
    pallas_call x2, Pallas kernels, attend_forward(): pl.pallas_call(partial(attend_forward_kernel, plan, len(arrays), merge is...  27.9 us
  transfers between devices with their start and end apart: 99, of which 34 were waited for; matrix products, arithmetic and copies ran while one was open for 10% of the time, Pallas kernels for 36%

profile of v1, /device:TPU:27, one launch (start us, length us, event | category | flops | bytes accessed | tf_op | source)
XLA Modules:
  0.0 643.1 jit_solution(764995423867363143)
XLA Ops:
  8.6 3.8 pack.4
  21.0 19.4 %collective-permute-done = f32[1,9344]{1,0:T(1,128)} collective-permute-done((f32[1,9344]{1,0:T(1,128)S(1)}, f32[1,9344]{1,0:T(1,128)}, u32[]{:S(2)}, u32[]{:S(2)}) %collective-permute-start) | collective-permute-done | bytes 37408 | tf_op jit(solution)/shard_map/ppermute | solution.py:914
  41.9 1.9 collective-permute-start.8
  43.9 3.7 pack.5
  54.0 22.9 %collective-permute-done.5.refs_6_.refs_5_ = bf16[2,384,768]{2,1,0:T(8,128)(2,1)} collective-permute-done((bf16[2,384,768]{2,1,0:T(8,128)(2,1)}, bf16[2,384,768]{2,1,0:T(8,128)(2,1)}, u32[]{:S(2)}, u32[]{:S(2)}) %collective-permute-start.5) | collective-permute-done | bytes 1179680 | tf_op jit(solution)/shard_map/ppermute | solution.py:914
  78.3 4.5 pack.6
  82.8 2.9 collective-permute-start.12
  90.9 5.0 collective-permute-start.18
  95.9 13.9 %attend_forward.2 = (f32[3,256,768]{2,1,0:T(8,128)}, bf16[3,256,2304]{2,1,0:T(8,128)(2,1)}, bf16[3,256,768]{2,1,0:T(8,128)(2,1)}, bf16[3,48,768]{2,1,0:T(8,128)(2,1)}) custom-call(s32[6]{0:T(128)} %pad_add_fusion.info, bf16[768,2304]{1,0:T(8,128)(2,1)} %bitcast.87, bf16[768,768]{1,0:T(8,128)(2,1)} %bitcast.100, bf16[768,3072]{1,0:T(8,128)(2,1)} %bitcast.59, ...), custom_call_target="tpu_custom_call" | custom-call | bytes 100000 | tf_op jit(solution)/shard_map/attend_forward/pallas_call | solution.py:380
  109.8 2.2 collective-permute-done.12.refs_6_.refs_8_.refs_14_
  113.7 2.9 collective-permute-start.14
  118.5 2.2 collective-permute-start.16
  120.7 4.5 pack.7
  129.3 2.4 collective-permute-start.20
  133.8 13.0 %shared_forward.1 = (bf16[144,768]{1,0:T(8,128)(2,1)}, bf16[144,768]{1,0:T(8,128)(2,1)}, bf16[144,768]{1,0:T(8,128)(2,1)}, bf16[144,768]{1,0:T(8,128)(2,1)}) custom-call(bf16[144,768]{1,0:T(8,128)(2,1)} %bitcast.114, bf16[144,768]{1,0:T(8,128)(2,1)} %collective-permute-done.14.refs_1_.refs_9_, bf16[144,768]{1,0:T(8,128)(2,1)} %collective-permute-done.15.refs_2_.refs_10_, ...), custom_call_target="tpu_custom_call" | custom-call | bytes 100000 | tf_op jit(solution)/shard_map/shared_forward/pallas_call | solution.py:739
  146.8 8.6 %collective-permute-done.19.refs_10_.refs_4_ = bf16[2,384,768]{2,1,0:T(8,128)(2,1)S(1)} collective-permute-done((bf16[2,384,768]{2,1,0:T(8,128)(2,1)}, bf16[2,384,768]{2,1,0:T(8,128)(2,1)S(1)}, u32[]{:S(2)}, u32[]{:S(2)}) %collective-permute-start.19) | collective-permute-done | bytes 1179680 | tf_op jit(solution)/shard_map/ppermute | solution.py:914
  157.3 2.4 collective-permute-done.21.refs_14_
  160.8 2.6 collective-permute-start.25
  170.4 19.9 %expert_forward_patch.1 = (bf16[3,256,768]{2,1,0:T(8,128)(2,1)}, bf16[624,3072]{1,0:T(8,128)(2,1)}, bf16[624,3072]{1,0:T(8,128)(2,1)}) custom-call(s32[6]{0:T(128)} %pad_add_fusion.info, bf16[768,2304]{1,0:T(8,128)(2,1)} %bitcast.89, bf16[768,768]{1,0:T(8,128)(2,1)} %bitcast.102, bf16[768,3072]{1,0:T(8,128)(2,1)} %bitcast.62, bf16[3072,768]{1,0:T(8,128)(2,1)} %bitcast.76, ...), custom_call_target="tpu_custom_call" | custom-call | bytes 100000 | tf_op jit(solution)/shard_map/expert_forward_patch/pallas_call | solution.py:656
  190.3 3.1 collective-permute-done.30.refs_16_
  198.6 1.9 collective-permute-done.34.refs_9_
  203.2 13.9 %attend_forward.3 = (bf16[3,256,768]{2,1,0:T(8,128)(2,1)}, bf16[3,256,2304]{2,1,0:T(8,128)(2,1)}, bf16[3,256,768]{2,1,0:T(8,128)(2,1)}, bf16[3,256,768]{2,1,0:T(8,128)(2,1)}) custom-call(s32[6]{0:T(128)} %pad_add_fusion.info, bf16[768,2304]{1,0:T(8,128)(2,1)} %bitcast.90, bf16[768,768]{1,0:T(8,128)(2,1)} %bitcast.103, bf16[768,3072]{1,0:T(8,128)(2,1)} %bitcast.63, ...), custom_call_target="tpu_custom_call" | custom-call | bytes 100000 | tf_op jit(solution)/shard_map/attend_forward/pallas_call | solution.py:380
  217.2 2.1 collective-permute-start.40
  219.3 21.6 %expert_forward_all.1 = (bf16[3,256,768]{2,1,0:T(8,128)(2,1)}, bf16[720,3072]{1,0:T(8,128)(2,1)}, bf16[720,3072]{1,0:T(8,128)(2,1)}) custom-call(s32[6]{0:T(128)} %pad_add_fusion.info, bf16[768,2304]{1,0:T(8,128)(2,1)} %bitcast.91, bf16[768,768]{1,0:T(8,128)(2,1)} %bitcast.104, bf16[768,3072]{1,0:T(8,128)(2,1)} %bitcast.64, bf16[3072,768]{1,0:T(8,128)(2,1)} %bitcast.78, ...), custom_call_target="tpu_custom_call" | custom-call | bytes 100000 | tf_op jit(solution)/shard_map/expert_forward_all/pallas_call | solution.py:656
  241.4 4.2 collective-permute-start.41
  245.7 27.0 %expert_backward_all.1 = (bf16[3,256,768]{2,1,0:T(8,128)(2,1)}, f32[1,768]{1,0:T(1,128)}, f32[1,768]{1,0:T(1,128)}, f32[1,3072]{1,0:T(1,128)}, f32[1,768]{1,0:T(...) custom-call(s32[6]{0:T(128)} %pad_add_fusion.info, ...), custom_call_target="tpu_custom_call" | custom-call | bytes 100000 | tf_op jit(solution)/shard_map/expert_backward_all/pallas_call | solution.py:692
  273.9 3.9 collective-permute-done.42
  277.7 3.9 add_convert_fusion.3
  281.6 2.7 collective-permute-start.43
  284.4 29.4 %attend_backward.2 = (bf16[3,256,768]{2,1,0:T(8,128)(2,1)}, f32[1,768]{1,0:T(1,128)}, f32[1,768]{1,0:T(1,128)}, f32[1,2304]{1,0:T(1,128)}, bf16[1,192,3072]{2,1,...) custom-call(s32[6]{0:T(128)} %pad_add_fusion.info, ...), custom_call_target="tpu_custom_call" | custom-call | flops 30000001024 | bytes 30000000 | tf_op jit(solution)/shard_map/attend_backward/pallas_call | solution.py:432
  316.5 2.7 add_convert_fusion.17
  321.2 27.9 %expert_backward_patch.1 = (bf16[3,256,768]{2,1,0:T(8,128)(2,1)}, f32[1,768]{1,0:T(1,128)}, f32[1,768]{1,0:T(1,128)}, f32[1,3072]{1,0:T(1,128)}, f32[1,768]{1,0:...) custom-call(s32[6]{0:T(128)} %pad_add_fusion.info, ...), custom_call_target="tpu_custom_call" | custom-call | bytes 100000 | tf_op jit(solution)/shard_map/expert_backward_patch/pallas_call | solution.py:692
  349.8 10.0 %shared_backward.1 = (bf16[144,768]{1,0:T(8,128)(2,1)}, bf16[144,768]{1,0:T(8,128)(2,1)}, bf16[144,768]{1,0:T(8,128)(2,1)}, bf16[144,768]{1,0:T(8,128)(2,1)}, bf...) custom-call(s32[6]{0:T(128)} %pad_add_fusion.info, ...), custom_call_target="tpu_custom_call" | custom-call | bytes 100000 | tf_op jit(solution)/shard_map/shared_backward/pallas_call | solution.py:762
  359.8 2.1 collective-permute-start.52
  366.3 3.0 add_convert_fusion.16
  374.9 2.7 add_convert_fusion.13
  381.6 30.6 %attend_backward.3 = (bf16[3,256,768]{2,1,0:T(8,128)(2,1)}, f32[1,768]{1,0:T(1,128)}, f32[1,768]{1,0:T(1,128)}, f32[1,2304]{1,0:T(1,128)}, bf16[1,192,3072]{2,1,...) custom-call(s32[6]{0:T(128)} %pad_add_fusion.info, ...), custom_call_target="tpu_custom_call" | custom-call | flops 30000001024 | bytes 30000000 | tf_op jit(solution)/shard_map/attend_backward/pallas_call | solution.py:432
  414.0 4.5 collective-permute-done.60
  425.4 2.1 collective-permute-start.65
  428.0 2.1 add_convert_fusion.11
  434.3 2.3 fusion.13
  438.9 9.7 %collective-permute-done.77 = bf16[2,48,3072]{2,1,0:T(8,128)(2,1)S(1)} collective-permute-done((bf16[2,48,3072]{2,1,0:T(8,128)(2,1)S(1)}, bf16[2,48,3072]{2,1,0:T(8,128)(2,1)S(1)}, u32[]{:S(2)}, u32[]{:S(2)}) %collective-permute-start.77) | collective-permute-done | bytes 589856 | tf_op jit(solution)/shard_map/ppermute | solution.py:914
  448.6 2.2 add_convert_fusion.8
  450.9 18.2 %all-reduce.5.cloned.1.call-done = bf16[4,96,3072]{2,1,0:T(8,128)(2,1)} async-done(((bf16[4,96,3072]{2,1,0:T(8,128)(2,1)}), bf16[4,96,3072]{2,1,0:T(8,128)(2,1)}) %all-reduce.5.cloned.1.call-update) | async-done | bytes 2359312 | tf_op jit(solution)/shard_map/psum | solution.py:1351
  476.3 7.3 %collective-permute-done.79 = bf16[2,96,1536]{2,1,0:T(8,128)(2,1)S(1)} collective-permute-done((bf16[2,96,1536]{2,1,0:T(8,128)(2,1)S(1)}, bf16[2,96,1536]{2,1,0:T(8,128)(2,1)S(1)}, u32[]{:S(2)}, u32[]{:S(2)}) %collective-permute-start.79) | collective-permute-done | bytes 589856 | tf_op jit(solution)/shard_map/ppermute | solution.py:922
  484.5 5.0 collective-permute-done.69
  489.6 2.3 fusion.7
  492.8 6.7 %collective-permute-done.80 = bf16[2,96,768]{2,1,0:T(8,128)(2,1)S(1)} collective-permute-done((bf16[2,96,768]{2,1,0:T(8,128)(2,1)S(1)}, bf16[2,96,768]{2,1,0:T(8,128)(2,1)S(1)}, u32[]{:S(2)}, u32[]{:S(2)}) %collective-permute-start.80) | collective-permute-done | bytes 294944 | tf_op jit(solution)/shard_map/ppermute | solution.py:922
  501.6 2.7 collective-permute-start.84
  504.3 6.0 collective-permute-done.81
  510.4 2.5 collective-permute-start.82
  512.9 6.6 %collective-permute-done.71 = bf16[200,1536]{1,0:T(8,128)(2,1)S(1)} collective-permute-done((bf16[200,1536]{1,0:T(8,128)(2,1)S(1)}, bf16[200,1536]{1,0:T(8,128)(2,1)S(1)}, u32[]{:S(2)}, u32[]{:S(2)}) %collective-permute-start.71) | collective-permute-done | bytes 614432 | tf_op jit(solution)/shard_map/ppermute | solution.py:922
  521.0 2.0 pad_maximum_fusion.13
  525.2 3.8 collective-permute-done.72
  529.1 2.6 collective-permute-start.73
  531.7 11.3 %collective-permute-done.82 = bf16[2,96,1536]{2,1,0:T(8,128)(2,1)S(1)} collective-permute-done((bf16[2,96,1536]{2,1,0:T(8,128)(2,1)S(1)}, bf16[2,96,1536]{2,1,0:T(8,128)(2,1)S(1)}, u32[]{:S(2)}, u32[]{:S(2)}) %collective-permute-start.82) | collective-permute-done | bytes 589856 | tf_op jit(solution)/shard_map/ppermute | solution.py:922
  547.7 2.6 collective-permute-done.73
  550.8 14.1 %collective-permute-done.74 = bf16[200,1536]{1,0:T(8,128)(2,1)S(1)} collective-permute-done((bf16[200,1536]{1,0:T(8,128)(2,1)S(1)}, bf16[200,1536]{1,0:T(8,128)(2,1)S(1)}, u32[]{:S(2)}, u32[]{:S(2)}) %collective-permute-start.74) | collective-permute-done | bytes 614432 | tf_op jit(solution)/shard_map/ppermute | solution.py:922
  568.0 4.1 collective-permute-done.85
  572.2 2.3 collective-permute-start.90
  576.0 22.6 %collective-permute-done.86 = bf16[2,96,3072]{2,1,0:T(8,128)(2,1)S(1)} collective-permute-done((bf16[2,96,3072]{2,1,0:T(8,128)(2,1)S(1)}, bf16[2,96,3072]{2,1,0:T(8,128)(2,1)S(1)}, u32[]{:S(2)}, u32[]{:S(2)}) %collective-permute-start.86) | collective-permute-done | bytes 1179680 | tf_op jit(solution)/shard_map/ppermute | solution.py:914
  602.4 2.2 collective-permute-start.93
  609.2 12.3 %finish.2 = (f32[1,768,3072]{2,1,0:T(8,128)}, f32[1,3072,768]{2,1,0:T(8,128)}) custom-call(s32[6]{0:T(128)} %pad_add_fusion.info, f32[1,1]{1,0:T(1,128)} %bitcast.29.scale_ref, bf16[2,96,3072]{2,1,0:T(8,128)(2,1)} %copy-done.15, bf16[2,96,3072]{2,1,0:T(8,128)(2,1)} %copy-done.16, bf16[2,96,3072]{2,1,0:T(8,128)(2,1)} %copy-done.17, ...), custom_call_target="tpu_custom_call" | custom-call | bytes 100000 | tf_op jit(solution)/shard_map/finish/pallas_call | solution.py:858
  627.4 8.6 %finish.3 = (f32[1,768,2304]{2,1,0:T(8,128)}, f32[1,768,768]{2,1,0:T(8,128)}) custom-call(s32[6]{0:T(128)} %pad_add_fusion.info, f32[1,1]{1,0:T(1,128)} %bitcast.25.scale_ref, bf16[1,96,3072]{2,1,0:T(8,128)(2,1)} %copy-done.23, bf16[1,96,3072]{2,1,0:T(8,128)(2,1)} %copy-done.19, bf16[1,96,3072]{2,1,0:T(8,128)(2,1)} %copy-done.20, ...), custom_call_target="tpu_custom_call" | custom-call | bytes 100000 | tf_op jit(solution)/shard_map/finish/pallas_call | solution.py:858
  (425 shorter events, 126.5 us)
Async XLA Ops:
  7.2 461.9 %all-reduce.5.cloned.1.call-start = ((), (), s32[]{:S(2)}) async-start(), calls=%async_computation | async-start | bytes 4718592 | tf_op jit(solution)/shard_map/psum | solution.py:1351
  12.5 29.4 %collective-permute-start.3 = (bf16[2,384,768]{2,1,0:T(8,128)(2,1)}, bf16[2,384,768]{2,1,0:T(8,128)(2,1)S(1)}, u32[]{:S(2)}, u32[]{:S(2)}) collective-permute-start(bf16[2,384,768]{2,1,0:T(8,128)(2,1)} %get-tuple-element.286), channel_id=1, source_target_pairs={{0,8},{8,0},{16,24},{24,16},{1,9},{9,1},{17,25},{25,17},{2,10},{10... | collective-permute-start | bytes 3538952 | tf_op jit(solution)/shard_map/ppermute | solution.py:914
  12.8 29.1 %collective-permute-start.4 = (bf16[2,384,768]{2,1,0:T(8,128)(2,1)}, bf16[2,384,768]{2,1,0:T(8,128)(2,1)S(1)}, u32[]{:S(2)}, u32[]{:S(2)}) collective-permute-start(bf16[2,384,768]{2,1,0:T(8,128)(2,1)} %get-tuple-element.287), channel_id=1, source_target_pairs={{0,16},{8,24},{16,0},{24,8},{1,17},{9,25},{17,1},{25,9},{2,18},{10... | collective-permute-start | bytes 3538952 | tf_op jit(solution)/shard_map/ppermute | solution.py:914
  15.5 24.9 %collective-permute-start = (f32[1,9344]{1,0:T(1,128)S(1)}, f32[1,9344]{1,0:T(1,128)}, u32[]{:S(2)}, u32[]{:S(2)}) collective-permute-start(f32[1,9344]{1,0:T(1,128)S(1)} %constant_dynamic-update-slice_fusion), channel_id=1, source_target_pairs={{0,8},{8,0},{16,24},{24,16},{1,9},{9,1},{17,25},{25,17},{2,10},{10... | collective-permute-start | bytes 112136 | tf_op jit(solution)/shard_map/ppermute | solution.py:914
  16.8 23.6 %collective-permute-start.1 = (f32[1,9344]{1,0:T(1,128)S(1)}, f32[1,9344]{1,0:T(1,128)}, u32[]{:S(2)}, u32[]{:S(2)}) collective-permute-start(f32[1,9344]{1,0:T(1,128)S(1)} %constant_dynamic-update-slice_fusion), channel_id=1, source_target_pairs={{0,16},{8,24},{16,0},{24,8},{1,17},{9,25},{17,1},{25,9},{2,18},{10... | collective-permute-start | bytes 112136 | tf_op jit(solution)/shard_map/ppermute | solution.py:914
  17.0 24.9 %collective-permute-start.2 = (f32[1,9344]{1,0:T(1,128)S(1)}, f32[1,9344]{1,0:T(1,128)}, u32[]{:S(2)}, u32[]{:S(2)}) collective-permute-start(f32[1,9344]{1,0:T(1,128)S(1)} %constant_dynamic-update-slice_fusion), channel_id=1, source_target_pairs={{0,24},{8,16},{16,8},{24,0},{1,25},{9,17},{17,9},{25,1},{2,26},{10... | collective-permute-start | bytes 112136 | tf_op jit(solution)/shard_map/ppermute | solution.py:914
  41.9 43.7 %collective-permute-start.8 = (bf16[2,384,768]{2,1,0:T(8,128)(2,1)S(1)}, bf16[2,384,768]{2,1,0:T(8,128)(2,1)S(1)}, u32[]{:S(2)}, u32[]{:S(2)}) collective-permute-start(bf16[2,384,768]{2,1,0:T(8,128)(2,1)S(1)} %collective-permute-done.3.refs_5_.refs_4_.refs_12_), channel_id=1, source_target_pairs={{0,1},{1,0},{2,3},{3,2},{4,5},{5,4},{6,7},{7,6},{8,9},{9,8},{10,11... | collective-permute-start | bytes 3538952 | tf_op jit(solution)/shard_map/ppermute | solution.py:918
  47.6 39.7 %collective-permute-start.9 = (bf16[2,384,768]{2,1,0:T(8,128)(2,1)}, bf16[2,384,768]{2,1,0:T(8,128)(2,1)}, u32[]{:S(2)}, u32[]{:S(2)}) collective-permute-start(bf16[2,384,768]{2,1,0:T(8,128)(2,1)} %copy-done.1), channel_id=1, source_target_pairs={{0,1},{1,0},{2,3},{3,2},{4,5},{5,4},{6,7},{7,6},{8,9},{9,8},{10,11... | collective-permute-start | bytes 3538952 | tf_op jit(solution)/shard_map/ppermute | solution.py:918
  49.0 27.9 %collective-permute-start.5 = (bf16[2,384,768]{2,1,0:T(8,128)(2,1)}, bf16[2,384,768]{2,1,0:T(8,128)(2,1)}, u32[]{:S(2)}, u32[]{:S(2)}) collective-permute-start(bf16[2,384,768]{2,1,0:T(8,128)(2,1)} %get-tuple-element.294), channel_id=1, source_target_pairs={{0,8},{8,0},{16,24},{24,16},{1,9},{9,1},{17,25},{25,17},{2,10},{10... | collective-permute-start | bytes 3538952 | tf_op jit(solution)/shard_map/ppermute | solution.py:914
  49.6 27.5 %collective-permute-start.6 = (bf16[2,384,768]{2,1,0:T(8,128)(2,1)}, bf16[2,384,768]{2,1,0:T(8,128)(2,1)}, u32[]{:S(2)}, u32[]{:S(2)}) collective-permute-start(bf16[2,384,768]{2,1,0:T(8,128)(2,1)} %get-tuple-element.295), channel_id=1, source_target_pairs={{0,16},{8,24},{16,0},{24,8},{1,17},{9,25},{17,1},{25,9},{2,18},{10... | collective-permute-start | bytes 3538952 | tf_op jit(solution)/shard_map/ppermute | solution.py:914
  82.8 29.2 %collective-permute-start.12 = (bf16[2,384,768]{2,1,0:T(8,128)(2,1)}, bf16[2,384,768]{2,1,0:T(8,128)(2,1)S(1)}, u32[]{:S(2)}, u32[]{:S(2)}) collective-permute-start(bf16[2,384,768]{2,1,0:T(8,128)(2,1)} %get-tuple-element.319), channel_id=1, source_target_pairs={{0,8},{8,0},{16,24},{1,9},{9,1},{17,25},{2,10},{10,2},{18,26},{3,1... | collective-permute-start | bytes 3538952 | tf_op jit(solution)/shard_map/ppermute | solution.py:914
  85.7 26.7 %collective-permute-start.13 = (bf16[2,384,768]{2,1,0:T(8,128)(2,1)}, bf16[2,384,768]{2,1,0:T(8,128)(2,1)S(1)}, u32[]{:S(2)}, u32[]{:S(2)}) collective-permute-start(bf16[2,384,768]{2,1,0:T(8,128)(2,1)} %get-tuple-element.320), channel_id=1, source_target_pairs={{0,16},{8,24},{16,0},{1,17},{9,25},{17,1},{2,18},{10,26},{18,2},{3... | collective-permute-start | bytes 3538952 | tf_op jit(solution)/shard_map/ppermute | solution.py:914
  89.0 29.5 %collective-permute-start.17 = (bf16[2,384,768]{2,1,0:T(8,128)(2,1)}, bf16[2,384,768]{2,1,0:T(8,128)(2,1)}, u32[]{:S(2)}, u32[]{:S(2)}) collective-permute-start(bf16[2,384,768]{2,1,0:T(8,128)(2,1)} %get-tuple-element.368.refs_4_), channel_id=1, source_target_pairs={{0,2},{2,4},{4,6},{1,3},{3,5},{5,7},{8,10},{10,12},{12,14},{9,11},... | collective-permute-start | bytes 3538952 | tf_op jit(solution)/shard_map/ppermute | solution.py:922
  90.9 34.3 %collective-permute-start.18 = (bf16[2,384,768]{2,1,0:T(8,128)(2,1)}, bf16[2,384,768]{2,1,0:T(8,128)(2,1)}, u32[]{:S(2)}, u32[]{:S(2)}) collective-permute-start(bf16[2,384,768]{2,1,0:T(8,128)(2,1)} %get-tuple-element.368.refs_4_), channel_id=1, source_target_pairs={{6,4},{4,2},{2,0},{7,5},{5,3},{3,1},{14,12},{12,10},{10,8},{15,13}... | collective-permute-start | bytes 3538952 | tf_op jit(solution)/shard_map/ppermute | solution.py:922
  112.4 20.6 %collective-permute-start.23 = (bf16[2,384,768]{2,1,0:T(8,128)(2,1)S(1)}, bf16[2,384,768]{2,1,0:T(8,128)(2,1)S(1)}, u32[]{:S(2)}, u32[]{:S(2)}) collective-permute-start(bf16[2,384,768]{2,1,0:T(8,128)(2,1)S(1)} %collective-permute-done.12.refs_6_.refs_8_.refs_14_), channel_id=1, source_target_pairs={{0,1},{1,0},{2,3},{3,2},{4,5},{5,4},{6,7},{7,6},{8,9},{9,8},{10,11... | collective-permute-start | bytes 3538952 | tf_op jit(solution)/shard_map/ppermute | solution.py:918
  125.2 21.6 %collective-permute-start.24 = (bf16[2,384,768]{2,1,0:T(8,128)(2,1)}, bf16[2,384,768]{2,1,0:T(8,128)(2,1)S(1)}, u32[]{:S(2)}, u32[]{:S(2)}) collective-permute-start(bf16[2,384,768]{2,1,0:T(8,128)(2,1)} %copy-done.3), channel_id=1, source_target_pairs={{0,1},{1,0},{2,3},{3,2},{4,5},{5,4},{6,7},{7,6},{8,9},{9,8},{10,11... | collective-permute-start | bytes 3538952 | tf_op jit(solution)/shard_map/ppermute | solution.py:918
  128.6 26.8 %collective-permute-start.19 = (bf16[2,384,768]{2,1,0:T(8,128)(2,1)}, bf16[2,384,768]{2,1,0:T(8,128)(2,1)S(1)}, u32[]{:S(2)}, u32[]{:S(2)}) collective-permute-start(bf16[2,384,768]{2,1,0:T(8,128)(2,1)} %get-tuple-element.341), channel_id=1, source_target_pairs={{0,8},{8,0},{16,24},{24,16},{1,9},{9,1},{17,25},{25,17},{2,10},{10... | collective-permute-start | bytes 3538952 | tf_op jit(solution)/shard_map/ppermute | solution.py:914
  129.3 28.0 %collective-permute-start.20 = (bf16[2,384,768]{2,1,0:T(8,128)(2,1)}, bf16[2,384,768]{2,1,0:T(8,128)(2,1)S(1)}, u32[]{:S(2)}, u32[]{:S(2)}) collective-permute-start(bf16[2,384,768]{2,1,0:T(8,128)(2,1)} %get-tuple-element.342), channel_id=1, source_target_pairs={{0,16},{8,24},{24,8},{1,17},{9,25},{25,9},{2,18},{10,26},{26,10},{... | collective-permute-start | bytes 3538952 | tf_op jit(solution)/shard_map/ppermute | solution.py:914
  131.7 28.0 %collective-permute-start.21 = (bf16[2,384,768]{2,1,0:T(8,128)(2,1)}, bf16[2,384,768]{2,1,0:T(8,128)(2,1)}, u32[]{:S(2)}, u32[]{:S(2)}) collective-permute-start(bf16[2,384,768]{2,1,0:T(8,128)(2,1)} %collective-permute-done.17.refs_12_), channel_id=1, source_target_pairs={{2,4},{4,6},{3,5},{5,7},{10,12},{12,14},{11,13},{13,15},{18,20},{2... | collective-permute-start | bytes 3538952 | tf_op jit(solution)/shard_map/ppermute | solution.py:922
  133.0 26.7 %collective-permute-start.22 = (bf16[2,384,768]{2,1,0:T(8,128)(2,1)}, bf16[2,384,768]{2,1,0:T(8,128)(2,1)S(1)}, u32[]{:S(2)}, u32[]{:S(2)}) collective-permute-start(bf16[2,384,768]{2,1,0:T(8,128)(2,1)} %collective-permute-done.18.refs_6_), channel_id=1, source_target_pairs={{4,2},{2,0},{5,3},{3,1},{12,10},{10,8},{13,11},{11,9},{20,18},{18,... | collective-permute-start | bytes 3538952 | tf_op jit(solution)/shard_map/ppermute | solution.py:922
  163.3 30.1 %collective-permute-start.30 = (bf16[2,384,768]{2,1,0:T(8,128)(2,1)}, bf16[2,384,768]{2,1,0:T(8,128)(2,1)}, u32[]{:S(2)}, u32[]{:S(2)}) collective-permute-start(bf16[2,384,768]{2,1,0:T(8,128)(2,1)} %collective-permute-done.21.refs_14_), channel_id=1, source_target_pairs={{4,6},{5,7},{12,14},{13,15},{20,22},{21,23},{28,30},{29,31}} | collective-permute-start | bytes 3538952 | tf_op jit(solution)/shard_map/ppermute | solution.py:922
  164.6 28.8 %collective-permute-start.31 = (bf16[2,384,768]{2,1,0:T(8,128)(2,1)}, bf16[2,384,768]{2,1,0:T(8,128)(2,1)}, u32[]{:S(2)}, u32[]{:S(2)}) collective-permute-start(bf16[2,384,768]{2,1,0:T(8,128)(2,1)} %copy-done.11), channel_id=1, source_target_pairs={{2,0},{3,1},{10,8},{11,9},{18,16},{19,17},{26,24},{27,25}} | collective-permute-start | bytes 3538952 | tf_op jit(solution)/shard_map/ppermute | solution.py:922
  166.3 24.0 %collective-permute-start.27 = (bf16[144,768]{1,0:T(8,128)(2,1)}, bf16[144,768]{1,0:T(8,128)(2,1)S(1)}, u32[]{:S(2)}, u32[]{:S(2)}) collective-permute-start(bf16[144,768]{1,0:T(8,128)(2,1)} %get-tuple-element.360), channel_id=1, source_target_pairs={{0,8},{1,9},{2,10},{3,11},{4,12},{5,13},{6,14},{7,15}} | collective-permute-start | bytes 663560 | tf_op jit(solution)/shard_map/ppermute | solution.py:914
  167.6 22.7 %collective-permute-start.28 = (bf16[144,768]{1,0:T(8,128)(2,1)}, bf16[144,768]{1,0:T(8,128)(2,1)}, u32[]{:S(2)}, u32[]{:S(2)}) collective-permute-start(bf16[144,768]{1,0:T(8,128)(2,1)} %get-tuple-element.361), channel_id=1, source_target_pairs={{0,16},{1,17},{2,18},{3,19},{4,20},{5,21},{6,22},{7,23}} | collective-permute-start | bytes 663560 | tf_op jit(solution)/shard_map/ppermute | solution.py:914
  169.0 21.3 %collective-permute-start.29 = (bf16[144,768]{1,0:T(8,128)(2,1)}, bf16[144,768]{1,0:T(8,128)(2,1)}, u32[]{:S(2)}, u32[]{:S(2)}) collective-permute-start(bf16[144,768]{1,0:T(8,128)(2,1)} %get-tuple-element.362), channel_id=1, source_target_pairs={{0,24},{1,25},{2,26},{3,27},{4,28},{5,29},{6,30},{7,31}} | collective-permute-start | bytes 663560 | tf_op jit(solution)/shard_map/ppermute | solution.py:914
  195.1 22.1 %collective-permute-start.35 = (bf16[2,384,768]{2,1,0:T(8,128)(2,1)}, bf16[2,384,768]{2,1,0:T(8,128)(2,1)S(1)}, u32[]{:S(2)}, u32[]{:S(2)}) collective-permute-start(bf16[2,384,768]{2,1,0:T(8,128)(2,1)} %collective-permute-done.18.refs_6_), channel_id=1, source_target_pairs={{0,1},{1,0},{2,3},{3,2},{4,5},{5,4},{6,7},{7,6},{8,9},{9,8},{10,11... | collective-permute-start | bytes 3538952 | tf_op jit(solution)/shard_map/ppermute | solution.py:918
  195.9 21.3 %collective-permute-start.36 = (bf16[2,384,768]{2,1,0:T(8,128)(2,1)}, bf16[2,384,768]{2,1,0:T(8,128)(2,1)}, u32[]{:S(2)}, u32[]{:S(2)}) collective-permute-start(bf16[2,384,768]{2,1,0:T(8,128)(2,1)} %get-tuple-element.368.refs_4_), channel_id=1, source_target_pairs={{0,1},{1,0},{2,3},{3,2},{4,5},{5,4},{6,7},{7,6},{8,9},{9,8},{10,11... | collective-permute-start | bytes 3538952 | tf_op jit(solution)/shard_map/ppermute | solution.py:918
  197.0 20.2 %collective-permute-start.37 = (bf16[2,384,768]{2,1,0:T(8,128)(2,1)}, bf16[2,384,768]{2,1,0:T(8,128)(2,1)}, u32[]{:S(2)}, u32[]{:S(2)}) collective-permute-start(bf16[2,384,768]{2,1,0:T(8,128)(2,1)} %collective-permute-done.17.refs_12_), channel_id=1, source_target_pairs={{0,1},{1,0},{2,3},{3,2},{4,5},{5,4},{6,7},{7,6},{8,9},{9,8},{10,11... | collective-permute-start | bytes 3538952 | tf_op jit(solution)/shard_map/ppermute | solution.py:918
  198.6 18.6 %collective-permute-start.38 = (bf16[2,384,768]{2,1,0:T(8,128)(2,1)}, bf16[2,384,768]{2,1,0:T(8,128)(2,1)}, u32[]{:S(2)}, u32[]{:S(2)}) collective-permute-start(bf16[2,384,768]{2,1,0:T(8,128)(2,1)} %collective-permute-done.21.refs_14_), channel_id=1, source_target_pairs={{0,1},{1,0},{2,3},{3,2},{4,5},{5,4},{6,7},{7,6},{8,9},{9,8},{10,11... | collective-permute-start | bytes 3538952 | tf_op jit(solution)/shard_map/ppermute | solution.py:918
  217.2 23.7 %collective-permute-start.40 = (f32[1,128]{1,0:T(1,128)S(1)}, f32[1,128]{1,0:T(1,128)S(1)}, u32[]{:S(2)}, u32[]{:S(2)}) collective-permute-start(f32[1,128]{1,0:T(1,128)S(1)} %add.246), channel_id=1, source_target_pairs={{0,4},{2,6},{4,0},{6,2},{1,5},{3,7},{5,1},{7,3},{8,12},{10,14},{12... | collective-permute-start | bytes 1544 | tf_op jit(solution)/shard_map/ppermute | solution.py:922
  241.4 31.2 %collective-permute-start.41 = (bf16[2,384,768]{2,1,0:T(8,128)(2,1)S(1)}, bf16[2,384,768]{2,1,0:T(8,128)(2,1)}, u32[]{:S(2)}, u32[]{:S(2)}) collective-permute-start(bf16[2,384,768]{2,1,0:T(8,128)(2,1)S(1)} %copy-done.75), channel_id=1, source_target_pairs={{0,16},{8,24},{1,17},{9,25},{2,18},{10,26},{3,19},{11,27},{4,20},{... | collective-permute-start | bytes 3538952 | tf_op jit(solution)/shard_map/ppermute | solution.py:914
  273.4 40.4 %collective-permute-start.45 = (bf16[2,192,3072]{2,1,0:T(8,128)(2,1)}, bf16[2,192,3072]{2,1,0:T(8,128)(2,1)S(1)}, u32[]{:S(2)}, u32[]{:S(2)}) collective-permute-start(bf16[2,192,3072]{2,1,0:T(8,128)(2,1)} %get-tuple-element.441), channel_id=1, source_target_pairs={{0,1},{1,0},{2,3},{3,2},{4,5},{5,4},{6,7},{7,6},{8,9},{9,8},{10,11... | collective-permute-start | bytes 7077896 | tf_op jit(solution)/shard_map/ppermute | solution.py:918
  273.4 40.3 %collective-permute-start.46 = (bf16[2,384,768]{2,1,0:T(8,128)(2,1)}, bf16[2,384,768]{2,1,0:T(8,128)(2,1)}, u32[]{:S(2)}, u32[]{:S(2)}) collective-permute-start(bf16[2,384,768]{2,1,0:T(8,128)(2,1)} %collective-permute-done.41.refs_6_), channel_id=1, source_target_pairs={{0,1},{1,0},{2,3},{3,2},{4,5},{5,4},{6,7},{7,6},{8,9},{9,8},{10,11... | collective-permute-start | bytes 3538952 | tf_op jit(solution)/shard_map/ppermute | solution.py:918
  281.6 32.1 %collective-permute-start.43 = (bf16[2,96,3072]{2,1,0:T(8,128)(2,1)}, bf16[2,96,3072]{2,1,0:T(8,128)(2,1)S(1)}, u32[]{:S(2)}, u32[]{:S(2)}) collective-permute-start(bf16[2,96,3072]{2,1,0:T(8,128)(2,1)} %get-tuple-element.574), channel_id=1, source_target_pairs={{0,8},{8,0},{16,24},{24,16},{1,9},{9,1},{17,25},{25,17},{2,10},{10... | collective-permute-start | bytes 3538952 | tf_op jit(solution)/shard_map/ppermute | solution.py:914
  284.3 29.4 %collective-permute-start.44 = (bf16[2,96,3072]{2,1,0:T(8,128)(2,1)}, bf16[2,96,3072]{2,1,0:T(8,128)(2,1)}, u32[]{:S(2)}, u32[]{:S(2)}) collective-permute-start(bf16[2,96,3072]{2,1,0:T(8,128)(2,1)} %get-tuple-element.573), channel_id=1, source_target_pairs={{0,16},{8,24},{16,0},{24,8},{1,17},{9,25},{17,1},{25,9},{2,18},{10... | collective-permute-start | bytes 3538952 | tf_op jit(solution)/shard_map/ppermute | solution.py:914
  313.8 35.3 %collective-permute-start.47 = (bf16[144,768]{1,0:T(8,128)(2,1)}, bf16[144,768]{1,0:T(8,128)(2,1)S(1)}, u32[]{:S(2)}, u32[]{:S(2)}) collective-permute-start(bf16[144,768]{1,0:T(8,128)(2,1)} %bitcast.118), channel_id=1, source_target_pairs={{0,8},{8,0},{16,24},{24,16},{1,9},{9,1},{17,25},{25,17},{2,10},{10... | collective-permute-start | bytes 663560 | tf_op jit(solution)/shard_map/ppermute | solution.py:914
  313.9 35.2 %collective-permute-start.48 = (bf16[144,768]{1,0:T(8,128)(2,1)}, bf16[144,768]{1,0:T(8,128)(2,1)}, u32[]{:S(2)}, u32[]{:S(2)}) collective-permute-start(bf16[144,768]{1,0:T(8,128)(2,1)} %bitcast.119), channel_id=1, source_target_pairs={{0,16},{8,24},{16,0},{24,8},{1,17},{9,25},{17,1},{25,9},{2,18},{10... | collective-permute-start | bytes 663560 | tf_op jit(solution)/shard_map/ppermute | solution.py:914
  315.3 33.9 %collective-permute-start.49 = (bf16[144,768]{1,0:T(8,128)(2,1)}, bf16[144,768]{1,0:T(8,128)(2,1)}, u32[]{:S(2)}, u32[]{:S(2)}) collective-permute-start(bf16[144,768]{1,0:T(8,128)(2,1)} %bitcast.120), channel_id=1, source_target_pairs={{0,24},{8,16},{16,8},{24,0},{1,25},{9,17},{17,9},{25,1},{2,26},{10... | collective-permute-start | bytes 663560 | tf_op jit(solution)/shard_map/ppermute | solution.py:914
  319.2 45.2 %collective-permute-start.50 = (bf16[2,48,3072]{2,1,0:T(8,128)(2,1)}, bf16[2,48,3072]{2,1,0:T(8,128)(2,1)}, u32[]{:S(2)}, u32[]{:S(2)}) collective-permute-start(bf16[2,48,3072]{2,1,0:T(8,128)(2,1)} %get-tuple-element.571), channel_id=1, source_target_pairs={{0,16},{8,24},{16,0},{24,8},{1,17},{9,25},{17,1},{25,9},{2,18},{10... | collective-permute-start | bytes 1769480 | tf_op jit(solution)/shard_map/ppermute | solution.py:914
  320.5 45.6 %collective-permute-start.51 = (bf16[2,48,3072]{2,1,0:T(8,128)(2,1)}, bf16[2,48,3072]{2,1,0:T(8,128)(2,1)}, u32[]{:S(2)}, u32[]{:S(2)}) collective-permute-start(bf16[2,48,3072]{2,1,0:T(8,128)(2,1)} %get-tuple-element.572), channel_id=1, source_target_pairs={{0,8},{8,0},{16,24},{24,16},{1,9},{9,1},{17,25},{25,17},{2,10},{10... | collective-permute-start | bytes 1769480 | tf_op jit(solution)/shard_map/ppermute | solution.py:914
  373.7 54.4 %collective-permute-start.63 = (bf16[2,192,3072]{2,1,0:T(8,128)(2,1)}, bf16[2,192,3072]{2,1,0:T(8,128)(2,1)}, u32[]{:S(2)}, u32[]{:S(2)}) collective-permute-start(bf16[2,192,3072]{2,1,0:T(8,128)(2,1)} %get-tuple-element.506), channel_id=1, source_target_pairs={{0,1},{1,0},{2,3},{3,2},{4,5},{5,4},{6,7},{7,6},{8,9},{9,8},{10,11... | collective-permute-start | bytes 7077896 | tf_op jit(solution)/shard_map/ppermute | solution.py:918
  378.6 33.6 %collective-permute-start.58 = (bf16[1,96,3072]{2,1,0:T(8,128)(2,1)}, bf16[1,96,3072]{2,1,0:T(8,128)(2,1)}, u32[]{:S(2)}, u32[]{:S(2)}) collective-permute-start(bf16[1,96,3072]{2,1,0:T(8,128)(2,1)} %get-tuple-element.489), channel_id=1, source_target_pairs={{0,8},{8,0},{16,24},{24,16},{1,9},{9,1},{17,25},{25,17},{2,10},{10... | collective-permute-start | bytes 1769480 | tf_op jit(solution)/shard_map/ppermute | solution.py:914
  380.1 34.0 %collective-permute-start.59 = (bf16[1,96,3072]{2,1,0:T(8,128)(2,1)}, bf16[1,96,3072]{2,1,0:T(8,128)(2,1)}, u32[]{:S(2)}, u32[]{:S(2)}) collective-permute-start(bf16[1,96,3072]{2,1,0:T(8,128)(2,1)} %get-tuple-element.490), channel_id=1, source_target_pairs={{0,16},{8,24},{16,0},{24,8},{1,17},{9,25},{17,1},{25,9},{2,18},{10... | collective-permute-start | bytes 1769480 | tf_op jit(solution)/shard_map/ppermute | solution.py:914
  380.3 38.2 %collective-permute-start.60 = (bf16[2,96,3072]{2,1,0:T(8,128)(2,1)S(1)}, bf16[2,96,3072]{2,1,0:T(8,128)(2,1)S(1)}, u32[]{:S(2)}, u32[]{:S(2)}) collective-permute-start(bf16[2,96,3072]{2,1,0:T(8,128)(2,1)S(1)} %get-tuple-element.484), channel_id=1, source_target_pairs={{0,8},{8,0},{16,24},{24,16},{1,9},{9,1},{17,25},{25,17},{2,10},{10... | collective-permute-start | bytes 3538952 | tf_op jit(solution)/shard_map/ppermute | solution.py:914
  380.4 38.9 %collective-permute-start.61 = (bf16[2,96,3072]{2,1,0:T(8,128)(2,1)S(1)}, bf16[2,96,3072]{2,1,0:T(8,128)(2,1)}, u32[]{:S(2)}, u32[]{:S(2)}) collective-permute-start(bf16[2,96,3072]{2,1,0:T(8,128)(2,1)S(1)} %get-tuple-element.485), channel_id=1, source_target_pairs={{0,16},{8,24},{16,0},{24,8},{1,17},{9,25},{17,1},{25,9},{2,18},{10... | collective-permute-start | bytes 3538952 | tf_op jit(solution)/shard_map/ppermute | solution.py:914
  412.3 21.8 %collective-permute-start.68 = (bf16[1,192,3072]{2,1,0:T(8,128)(2,1)}, bf16[1,192,3072]{2,1,0:T(8,128)(2,1)}, u32[]{:S(2)}, u32[]{:S(2)}) collective-permute-start(bf16[1,192,3072]{2,1,0:T(8,128)(2,1)} %get-tuple-element.533), channel_id=1, source_target_pairs={{0,1},{1,0},{2,3},{3,2},{4,5},{5,4},{6,7},{7,6},{8,9},{9,8},{10,11... | collective-permute-start | bytes 3538952 | tf_op jit(solution)/shard_map/ppermute | solution.py:918
  427.6 43.8 %collective-permute-start.62 = (bf16[1,192,3072]{2,1,0:T(8,128)(2,1)}, bf16[1,192,3072]{2,1,0:T(8,128)(2,1)}, u32[]{:S(2)}, u32[]{:S(2)}) collective-permute-start(bf16[1,192,3072]{2,1,0:T(8,128)(2,1)} %get-tuple-element.504), channel_id=1, source_target_pairs={{0,1},{1,0},{2,3},{3,2},{4,5},{5,4},{6,7},{7,6},{8,9},{9,8},{10,11... | collective-permute-start | bytes 3538952 | tf_op jit(solution)/shard_map/ppermute | solution.py:918
  436.6 33.6 %collective-permute-start.66 = (bf16[104,3072]{1,0:T(8,128)(2,1)}, bf16[104,3072]{1,0:T(8,128)(2,1)}, u32[]{:S(2)}, u32[]{:S(2)}) collective-permute-start(bf16[104,3072]{1,0:T(8,128)(2,1)} %pad_maximum_fusion.4), channel_id=1, source_target_pairs={{0,8},{8,0},{16,24},{24,16},{1,9},{9,1},{17,25},{25,17},{2,10},{10... | collective-permute-start | bytes 1916936 | tf_op jit(solution)/shard_map/ppermute | solution.py:914
  437.7 33.7 %collective-permute-start.67 = (bf16[1,96,3072]{2,1,0:T(8,128)(2,1)}, bf16[1,96,3072]{2,1,0:T(8,128)(2,1)}, u32[]{:S(2)}, u32[]{:S(2)}) collective-permute-start(bf16[1,96,3072]{2,1,0:T(8,128)(2,1)} %get-tuple-element.530), channel_id=1, source_target_pairs={{0,16},{8,24},{16,0},{24,8},{1,17},{9,25},{17,1},{25,9},{2,18},{10... | collective-permute-start | bytes 1769480 | tf_op jit(solution)/shard_map/ppermute | solution.py:914
  492.1 27.4 %collective-permute-start.71 = (bf16[200,1536]{1,0:T(8,128)(2,1)S(1)}, bf16[200,1536]{1,0:T(8,128)(2,1)S(1)}, u32[]{:S(2)}, u32[]{:S(2)}) collective-permute-start(bf16[200,1536]{1,0:T(8,128)(2,1)S(1)} %constant_dynamic-slice_fusion.8), channel_id=1, source_target_pairs={{0,2},{2,0},{4,6},{6,4},{1,3},{3,1},{5,7},{7,5},{8,10},{10,8},{12,... | collective-permute-start | bytes 1843208 | tf_op jit(solution)/shard_map/ppermute | solution.py:922
  499.9 43.2 %collective-permute-start.83 = (bf16[2,96,3072]{2,1,0:T(8,128)(2,1)S(1)}, bf16[2,96,3072]{2,1,0:T(8,128)(2,1)S(1)}, u32[]{:S(2)}, u32[]{:S(2)}) collective-permute-start(bf16[2,96,3072]{2,1,0:T(8,128)(2,1)S(1)} %get-tuple-element.577), channel_id=1, source_target_pairs={{8,0},{16,24},{9,1},{17,25},{10,2},{18,26},{11,3},{19,27},{12,4},{... | collective-permute-start | bytes 3538952 | tf_op jit(solution)/shard_map/ppermute | solution.py:914
  501.6 41.4 %collective-permute-start.84 = (bf16[2,96,3072]{2,1,0:T(8,128)(2,1)S(1)}, bf16[2,96,3072]{2,1,0:T(8,128)(2,1)S(1)}, u32[]{:S(2)}, u32[]{:S(2)}) collective-permute-start(bf16[2,96,3072]{2,1,0:T(8,128)(2,1)S(1)} %get-tuple-element.576), channel_id=1, source_target_pairs={{8,24},{16,0},{9,25},{17,1},{10,26},{18,2},{11,27},{19,3},{12,28},... | collective-permute-start | bytes 3538952 | tf_op jit(solution)/shard_map/ppermute | solution.py:914
  510.4 32.5 %collective-permute-start.82 = (bf16[2,96,1536]{2,1,0:T(8,128)(2,1)S(1)}, bf16[2,96,1536]{2,1,0:T(8,128)(2,1)S(1)}, u32[]{:S(2)}, u32[]{:S(2)}) collective-permute-start(bf16[2,96,1536]{2,1,0:T(8,128)(2,1)S(1)} %pad_maximum_fusion.11), channel_id=1, source_target_pairs={{0,2},{2,0},{4,6},{6,4},{1,3},{3,1},{5,7},{7,5},{8,10},{10,8},{12,... | collective-permute-start | bytes 1769480 | tf_op jit(solution)/shard_map/ppermute | solution.py:922
  529.1 21.3 %collective-permute-start.73 = (bf16[200,768]{1,0:T(8,128)(2,1)S(1)}, bf16[200,768]{1,0:T(8,128)(2,1)S(1)}, u32[]{:S(2)}, u32[]{:S(2)}) collective-permute-start(bf16[200,768]{1,0:T(8,128)(2,1)S(1)} %add_convert_fusion.19), channel_id=1, source_target_pairs={{0,4},{2,6},{4,0},{6,2},{1,5},{3,7},{5,1},{7,3},{8,12},{10,14},{12... | collective-permute-start | bytes 921608 | tf_op jit(solution)/shard_map/ppermute | solution.py:922
  543.1 28.9 %collective-permute-start.85 = (bf16[2,96,3072]{2,1,0:T(8,128)(2,1)S(1)}, bf16[2,96,3072]{2,1,0:T(8,128)(2,1)S(1)}, u32[]{:S(2)}, u32[]{:S(2)}) collective-permute-start(bf16[2,96,3072]{2,1,0:T(8,128)(2,1)S(1)} %pad_maximum_fusion.3), channel_id=1, source_target_pairs={{0,8},{1,9},{2,10},{3,11},{4,12},{5,13},{6,14},{7,15}} | collective-permute-start | bytes 3538952 | tf_op jit(solution)/shard_map/ppermute | solution.py:914
  544.4 54.2 %collective-permute-start.86 = (bf16[2,96,3072]{2,1,0:T(8,128)(2,1)S(1)}, bf16[2,96,3072]{2,1,0:T(8,128)(2,1)S(1)}, u32[]{:S(2)}, u32[]{:S(2)}) collective-permute-start(bf16[2,96,3072]{2,1,0:T(8,128)(2,1)S(1)} %pad_maximum_fusion.3), channel_id=1, source_target_pairs={{24,8},{25,9},{26,10},{27,11},{28,12},{29,13},{30,14},{31,15}} | collective-permute-start | bytes 3538952 | tf_op jit(solution)/shard_map/ppermute | solution.py:914
  545.7 58.9 %collective-permute-start.88 = (bf16[2,96,3072]{2,1,0:T(8,128)(2,1)S(1)}, bf16[2,96,3072]{2,1,0:T(8,128)(2,1)S(1)}, u32[]{:S(2)}, u32[]{:S(2)}) collective-permute-start(bf16[2,96,3072]{2,1,0:T(8,128)(2,1)S(1)} %pad_maximum_fusion.3), channel_id=1, source_target_pairs={{16,8},{17,9},{18,10},{19,11},{20,12},{21,13},{22,14},{23,15}} | collective-permute-start | bytes 3538952 | tf_op jit(solution)/shard_map/ppermute | solution.py:914
  547.0 55.4 %collective-permute-start.87 = (bf16[2,96,3072]{2,1,0:T(8,128)(2,1)S(1)}, bf16[2,96,3072]{2,1,0:T(8,128)(2,1)S(1)}, u32[]{:S(2)}, u32[]{:S(2)}) collective-permute-start(bf16[2,96,3072]{2,1,0:T(8,128)(2,1)S(1)} %get-tuple-element.548), channel_id=1, source_target_pairs={{0,24},{24,0},{1,25},{25,1},{2,26},{26,2},{3,27},{27,3},{4,28},{28... | collective-permute-start | bytes 3538952 | tf_op jit(solution)/shard_map/ppermute | solution.py:914
  572.2 27.3 %collective-permute-start.90 = (bf16[2,96,3072]{2,1,0:T(8,128)(2,1)S(1)}, bf16[2,96,3072]{2,1,0:T(8,128)(2,1)S(1)}, u32[]{:S(2)}, u32[]{:S(2)}) collective-permute-start(bf16[2,96,3072]{2,1,0:T(8,128)(2,1)S(1)} %select_select_fusion.2.refs_1_), channel_id=1, source_target_pairs={{0,1},{1,0},{2,3},{3,2},{4,5},{5,4},{6,7},{7,6},{8,9},{9,8},{10,11... | collective-permute-start | bytes 3538952 | tf_op jit(solution)/shard_map/ppermute | solution.py:918
  574.6 30.2 %collective-permute-start.75 = (bf16[1,96,3072]{2,1,0:T(8,128)(2,1)S(1)}, bf16[1,96,3072]{2,1,0:T(8,128)(2,1)S(1)}, u32[]{:S(2)}, u32[]{:S(2)}) collective-permute-start(bf16[1,96,3072]{2,1,0:T(8,128)(2,1)S(1)} %get-tuple-element.595), channel_id=1, source_target_pairs={{8,0},{24,16},{9,1},{25,17},{10,2},{26,18},{11,3},{27,19},{12,4},{... | collective-permute-start | bytes 1769480 | tf_op jit(solution)/shard_map/ppermute | solution.py:914
  602.4 19.1 %collective-permute-start.93 = (bf16[1,96,3072]{2,1,0:T(8,128)(2,1)}, bf16[1,96,3072]{2,1,0:T(8,128)(2,1)}, u32[]{:S(2)}, u32[]{:S(2)}) collective-permute-start(bf16[1,96,3072]{2,1,0:T(8,128)(2,1)} %get-tuple-element.558), channel_id=1, source_target_pairs={{8,16},{24,0},{9,17},{25,1},{10,18},{26,2},{11,19},{27,3},{12,20},... | collective-permute-start | bytes 1769480 | tf_op jit(solution)/shard_map/ppermute | solution.py:914
  604.5 21.5 %collective-permute-start.94 = (bf16[1,96,3072]{2,1,0:T(8,128)(2,1)S(1)}, bf16[1,96,3072]{2,1,0:T(8,128)(2,1)S(1)}, u32[]{:S(2)}, u32[]{:S(2)}) collective-permute-start(bf16[1,96,3072]{2,1,0:T(8,128)(2,1)S(1)} %get-tuple-element.596.refs_0_), channel_id=1, source_target_pairs={{0,1},{1,0},{2,3},{3,2},{4,5},{5,4},{6,7},{7,6},{8,9},{9,8},{10,11... | collective-permute-start | bytes 1769480 | tf_op jit(solution)/shard_map/ppermute | solution.py:918
  605.4 20.6 %collective-permute-start.95 = (bf16[1,96,3072]{2,1,0:T(8,128)(2,1)S(1)}, bf16[1,96,3072]{2,1,0:T(8,128)(2,1)S(1)}, u32[]{:S(2)}, u32[]{:S(2)}) collective-permute-start(bf16[1,96,3072]{2,1,0:T(8,128)(2,1)S(1)} %fusion.2.refs_1_), channel_id=1, source_target_pairs={{0,1},{1,0},{2,3},{3,2},{4,5},{5,4},{6,7},{7,6},{8,9},{9,8},{10,11... | collective-permute-start | bytes 1769480 | tf_op jit(solution)/shard_map/ppermute | solution.py:918
  606.2 19.8 %collective-permute-start.96 = (bf16[1,96,3072]{2,1,0:T(8,128)(2,1)S(1)}, bf16[1,96,3072]{2,1,0:T(8,128)(2,1)S(1)}, u32[]{:S(2)}, u32[]{:S(2)}) collective-permute-start(bf16[1,96,3072]{2,1,0:T(8,128)(2,1)S(1)} %fusion.3.refs_2_), channel_id=1, source_target_pairs={{0,1},{1,0},{2,3},{3,2},{4,5},{5,4},{6,7},{7,6},{8,9},{9,8},{10,11... | collective-permute-start | bytes 1769480 | tf_op jit(solution)/shard_map/ppermute | solution.py:918
  (114 other events, 1497.2 us)
Sparse Core Ops, SparseCore 0:
  373.8 95.2 all-reduce.4
